TPU v7x, 256 devices: a whole 4x4x8 slice. The times are simulated.
256 devices in a mesh: tok: 64 (over z, y, core), head: 4 (over x).
Axes of the slice: x: 4, y: 4, z: 8, core: 2. Of those that a mesh axis runs over, the one named last changes fastest.
Arguments:
- tokens: bfloat16 [524288, 256], P('tok'), may hold values from -6 to 6
- coords: float32 [3, 524288], P(None, 'tok'), may hold values from -1 to 1, as said below
- latents: bfloat16 [256, 512], replicated, may hold values from -6 to 6
- anchors: float32 [3, 256], replicated, may hold values from -8 to 8
- gamma: float32 [8], P('head'), may hold values from 0.02 to 3
- w_query: bfloat16 [512, 512], P(None, 'head'), may hold values from -0.25 to 0.25
- w_key: bfloat16 [256, 512], P(None, 'head'), may hold values from -0.375 to 0.375
- w_value: bfloat16 [256, 512], P(None, 'head'), may hold values from -0.375 to 0.375
- w_out: bfloat16 [512, 512], P('head'), may hold values from -0.5 to 0.5
- d_update: bfloat16 [256, 512], replicated, may hold values from -6 to 6
Outputs:
- update: bfloat16 [256, 512], replicated
- d_latents: float32 [256, 512], replicated
- d_wq: float32 [512, 512], P(None, 'head')
- d_wk: float32 [256, 512], P(None, 'head')
- d_wv: float32 [256, 512], P(None, 'head')
- d_wo: float32 [512, 512], P('head')
Inputs may be any that keep to these rules, and one draw needn't show every extreme that they name: `coords`: x and y are spread over the box; the third coordinate rises with the token index.
All inputs are finite; a program needn't handle non-finite values.
Results may differ from a plain program's by a relative error of at most 0.013.
Values may be sent and summed in bfloat16 or wider, within the bound.
No kernel may reach another device: no remote copies, remote signals or barrier semaphores. Data moves between devices by JAX's collectives and lax.ppermute only.
A program may use at most 128 MiB of HBM per device.

v0:
```python
import jax
import jax.numpy as jnp
from jax import lax
from jax.sharding import PartitionSpec as P

HEAD_FEATURES = 64


def layer_norm(input_rows):
    row_average = jnp.mean(input_rows, axis=-1, keepdims=True)
    var = jnp.mean((input_rows - row_average) ** 2, axis=-1, keepdims=True)
    return (input_rows - row_average) * lax.rsqrt(var + 1e-05)


def norm_back(input_rows, upstream_gradient):
    row_average = jnp.mean(input_rows, axis=-1, keepdims=True)
    var = jnp.mean((input_rows - row_average) ** 2, axis=-1, keepdims=True)
    inverse_stddev = lax.rsqrt(var + 1e-05)
    normalized_input = (input_rows - row_average) * inverse_stddev
    return inverse_stddev * (
        upstream_gradient
        - jnp.mean(upstream_gradient, axis=-1, keepdims=True)
        - normalized_input * jnp.mean(upstream_gradient * normalized_input, axis=-1, keepdims=True)
    )


def spread(stat, head_size):
    return jnp.repeat(stat.T, head_size, axis=1)


def shards(tokens, coords, latents, anchors, gamma, w_query, w_key, w_value, w_out, d_update):
    f32 = jnp.float32
    bf16 = jnp.bfloat16
    scale = HEAD_FEATURES ** (-0.5)
    lat_rows = latents.shape[0]
    tok_rows = tokens.shape[0]
    local_heads = gamma.shape[0]
    local_width = w_query.shape[1]
    head_size = local_width // local_heads
    lat_norm = layer_norm(latents.astype(f32)).astype(bf16)
    query = (jnp.dot(lat_norm, w_query, preferred_element_type=f32) * scale).astype(bf16)
    q_heads = query.reshape(lat_rows, local_heads, head_size)
    tok_norm = layer_norm(tokens.astype(f32)).astype(bf16)
    anchor_sq = jnp.sum(anchors * anchors, axis=0)
    block = min(1024, tok_rows)
    steps_all = jnp.arange(tok_rows // block, dtype=jnp.int32)

    def tile(index):
        start = index * block
        tok_block = lax.dynamic_slice_in_dim(tok_norm, start, block, 0)
        points = lax.dynamic_slice_in_dim(coords, start, block, 1)
        keys = (
            jnp.dot(tok_block, w_key, preferred_element_type=f32)
            .astype(bf16)
            .reshape(block, local_heads, head_size)
        )
        values = (
            jnp.dot(tok_block, w_value, preferred_element_type=f32)
            .astype(bf16)
            .reshape(block, local_heads, head_size)
        )
        cross = jnp.dot(anchors.T, points, precision=lax.Precision.HIGHEST)
        dist = anchor_sq[:, None] + jnp.sum(points * points, axis=0)[None, :] - 2.0 * cross
        scores = (
            jnp.einsum("lhd,bhd->hlb", q_heads, keys, preferred_element_type=f32)
            - gamma[:, None, None] * dist[None]
        )
        return (tok_block, keys, values, scores)

    def forward_step(carry, index):
        run_max, total, accum = carry
        tok_block, keys, values, scores = tile(index)
        new_max = jnp.maximum(run_max, jnp.max(scores, axis=2))
        factor = jnp.exp(run_max - new_max)
        expo = jnp.exp(scores - new_max[:, :, None]).astype(bf16)
        total = total * factor + jnp.sum(expo.astype(f32), axis=2)
        weighted = jnp.einsum("hlb,bhd->lhd", expo, values, preferred_element_type=f32).reshape(
            lat_rows, local_width
        )
        accum = accum * spread(factor, head_size) + weighted
        return ((new_max, total, accum), None)

    init = (
        jnp.full((local_heads, lat_rows), -jnp.inf, f32),
        jnp.zeros((local_heads, lat_rows), f32),
        jnp.zeros((lat_rows, local_width), f32),
    )
    (row_max, total, accum), _ = lax.scan(forward_step, init, steps_all)
    global_max = lax.pmax(row_max, "tok")
    factor = jnp.exp(row_max - global_max)
    total, accum = lax.psum((total * factor, accum * spread(factor, head_size)), "tok")
    row_max = global_max
    attn = (accum / spread(total, head_size)).astype(bf16)
    update = (
        lax.psum(jnp.dot(attn, w_out, preferred_element_type=f32).astype(jnp.bfloat16), "head")
        .astype(jnp.float32)
        .astype(bf16)
    )
    d_attn = jnp.dot(d_update, w_out.T, preferred_element_type=f32).astype(bf16)
    d_wo = lax.dot_general(attn, d_update, (((0,), (0,)), ((), ())), preferred_element_type=f32)
    do_heads = d_attn.reshape(lat_rows, local_heads, head_size)
    delta = jnp.sum(
        (d_attn.astype(f32) * attn.astype(f32)).reshape(lat_rows, local_heads, head_size), axis=2
    ).T
    lse = row_max + jnp.log(total)

    def backward_step(carry, index):
        query_gradient, d_key_w, d_value_w = carry
        tok_block, keys, values, scores = tile(index)
        probs = jnp.exp(scores - lse[:, :, None])
        d_probs = jnp.einsum("lhd,bhd->hlb", do_heads, values, preferred_element_type=f32)
        d_scores = (probs * (d_probs - delta[:, :, None])).astype(bf16)
        probs_b = probs.astype(bf16)
        query_gradient = query_gradient + jnp.einsum(
            "hlb,bhd->lhd", d_scores, keys, preferred_element_type=f32
        ).reshape(lat_rows, local_width)
        d_keys = (
            jnp.einsum("hlb,lhd->bhd", d_scores, q_heads, preferred_element_type=f32)
            .reshape(block, local_width)
            .astype(bf16)
        )
        d_values = (
            jnp.einsum("hlb,lhd->bhd", probs_b, do_heads, preferred_element_type=f32)
            .reshape(block, local_width)
            .astype(bf16)
        )
        contract = (((0,), (0,)), ((), ()))
        d_key_w = d_key_w + lax.dot_general(tok_block, d_keys, contract, preferred_element_type=f32)
        d_value_w = d_value_w + lax.dot_general(
            tok_block, d_values, contract, preferred_element_type=f32
        )
        return ((query_gradient, d_key_w, d_value_w), None)

    feat = tokens.shape[1]
    init_back = (
        jnp.zeros((lat_rows, local_width), f32),
        jnp.zeros((feat, local_width), f32),
        jnp.zeros((feat, local_width), f32),
    )
    (query_gradient, d_wk, d_wv), _ = lax.scan(backward_step, init_back, steps_all)
    query_gradient, d_wk, d_wv = lax.psum((query_gradient, d_wk, d_wv), "tok")
    dq_b = (query_gradient * scale).astype(bf16)
    d_wq = lax.dot_general(lat_norm, dq_b, (((0,), (0,)), ((), ())), preferred_element_type=f32)
    d_norm = lax.psum(
        jnp.dot(dq_b, w_query.T, preferred_element_type=f32).astype(jnp.bfloat16), "head"
    ).astype(jnp.float32)
    d_latents = norm_back(latents.astype(f32), d_norm)
    return (update, d_latents, d_wq, d_wk, d_wv, d_wo)


def solution(mesh):
    return jax.shard_map(
        shards,
        mesh=mesh,
        in_specs=(
            P("tok", None),
            P(None, "tok"),
            P(),
            P(),
            P("head"),
            P(None, "head"),
            P(None, "head"),
            P(None, "head"),
            P("head", None),
            P(),
        ),
        out_specs=(P(), P(), P(None, "head"), P(None, "head"), P(None, "head"), P("head", None)),
        check_vma=False,
    )
```

profile of v0, /device:TPU:1, one launch (start us, length us, event | category | flops | bytes accessed | tf_op | source)
XLA Modules:
  0.0 792.0 jit_solution(12666772796756054754)
XLA Ops:
  9.5 3.5 convert_reduce_fusion.1
  13.1 2.5 fusion.30
  15.6 5.3 fusion.31
  21.8 85.6 %while.30 = (s32[]{:T(128)}, f32[2,256]{1,0:T(2,128)S(1)}, f32[2,256]{1,0:T(2,128)}, f32[256,128]{0,1:T(8,128)}, s32[8]{0:T(128)}, /*index=5*/bf16[8192,256]{1,0...) while((s32[]{:T(128)}, f32[2,256]{1,0:T(2,128)S(1)}, ...), condition=%wide.region_9.10_spmd.clone, body=%wide.region_5.9_spmd.clone.sunk | while | flops 283746304 | bytes 13654415 | solution.py:88
  107.5 128.3 %pmax.7 = f32[2,256]{1,0:T(2,128)S(1)} all-reduce(f32[2,256]{1,0:T(2,128)S(1)} %get-tuple-element.160), channel_id=1, replica_groups=mesh['tok'=64,'head'=4] {'tok'}, use_global_device_ids=true, to_apply=%region_10.11 | all-reduce | flops 512 | bytes 4096 | tf_op jit(solution)/shard_map/pmax | solution.py:89
  238.1 128.4 %psum.50 = f32[2,256]{1,0:T(2,128)S(1)} all-reduce(f32[2,256]{1,0:T(2,128)S(1)} %get-tuple-element.331), channel_id=1, replica_groups=mesh['tok'=64,'head'=4] {'tok'}, use_global_device_ids=true, to_apply=%region_12.13 | all-reduce | flops 512 | bytes 4096 | tf_op jit(solution)/shard_map/psum | solution.py:91
  366.5 44.0 %all-reduce.6.cloned.1.call-done = f32[256,128]{0,1:T(8,128)} async-done(((f32[256,128]{0,1:T(8,128)}), f32[256,128]{0,1:T(8,128)}) %all-reduce.6.cloned.1.call-update) | async-done | bytes 131088 | tf_op jit(solution)/shard_map/psum | solution.py:91
  412.7 140.6 %while.31 = (s32[]{:T(128)}, f32[256,128]{0,1:T(8,128)}, f32[256,128]{1,0:T(8,128)}, f32[256,128]{1,0:T(8,128)}, s32[8]{0:T(128)}, /*index=5*/bf16[8192,256]{1,0...) while((s32[]{:T(128)}, f32[256,128]{0,1:T(8,128)}, ...), condition=%wide.region_17.18_spmd.clone, body=%wide.region_15.17_spmd.clone.sunk | while | flops 618599424 | bytes 19313032 | solution.py:140
  415.3 1.8 fusion.157
  422.9 2.1 convolution_add_fusion.4
  427.4 2.0 convolution_add_fusion.5
  439.6 2.1 convolution_add_fusion.4
  445.1 2.1 convolution_add_fusion.5
  449.7 1.8 fusion.157
  457.3 2.1 convolution_add_fusion.4
  462.8 2.1 convolution_add_fusion.5
  475.0 2.1 convolution_add_fusion.4
  480.5 2.1 convolution_add_fusion.5
  492.7 2.1 convolution_add_fusion.4
  498.2 2.1 convolution_add_fusion.5
  510.4 2.1 convolution_add_fusion.4
  515.8 2.1 convolution_add_fusion.5
  528.1 2.1 convolution_add_fusion.4
  533.5 2.1 convolution_add_fusion.5
  545.8 2.1 convolution_add_fusion.4
  551.2 2.1 convolution_add_fusion.5
  553.4 1.9 convolution_convert_fusion.7
  555.3 174.8 %all-reduce.8.cloned.1.call-done = (f32[256,128]{0,1:T(8,128)}, f32[256,128]{1,0:T(8,128)}, f32[256,128]{1,0:T(8,128)}) async-done(((f32[256,128]{0,1:T(8,128)}, f32[256,128]{1,0:T(8,128)}, f32[256,128]{1,0:T(8,128)}), (f32[256,128]{0,1:T(8,128)}, f32[256,128]{1,0:T(8,128)}, f32[256,128]{1,0:T(8,128)})) %all-reduce.8.cloned.1.call-update) | async-done | bytes 393232 | tf_op jit(solution)/shard_map/psum | solution.py:141
  730.1 2.0 convolution_convert_fusion.6
  733.8 2.0 fusion.42
  735.8 43.4 %all-reduce.10.cloned.1.call-done = (bf16[256,512]{1,0:T(8,128)(2,1)}, bf16[256,512]{1,0:T(8,128)(2,1)}) async-done(((bf16[256,512]{1,0:T(8,128)(2,1)}, bf16[256,512]{1,0:T(8,128)(2,1)}), (bf16[256,512]{1,0:T(8,128)(2,1)}, bf16[256,512]{1,0:T(8,128)(2,1)})) %all-reduce.10.cloned.1.call-update) | async-done | bytes 524304 | tf_op jit(solution)/shard_map/psum | solution.py:95
  780.5 2.0 fusion.38
  (384 shorter events, 190.6 us)
Async XLA Ops:
  7.2 403.3 %copy-start = (bf16[256,512]{1,0:T(8,128)(2,1)S(1)}, bf16[256,512]{1,0:T(8,128)(2,1)}, u32[]{:S(2)}) copy-start(bf16[256,512]{1,0:T(8,128)(2,1)} %param.23) | copy-start | bytes 786436
  7.2 403.3 %all-reduce.6.cloned.1.call-start = ((), (), s32[]{:S(2)}) async-start(), calls=%async_computation | async-start | bytes 262144 | tf_op jit(solution)/shard_map/psum | solution.py:91
  8.3 12.6 %copy-start.18 = (f32[256]{0:T(256)}, f32[256]{0:T(256)S(1)}, u32[]{:S(2)}) copy-start(f32[256]{0:T(256)S(1)} %broadcast_multiply_fusion.3) | copy-start | bytes 3076
  9.5 11.4 %copy-start.20 = (f32[256]{0:T(256)}, f32[256]{0:T(256)S(1)}, u32[]{:S(2)}) copy-start(f32[256]{0:T(256)S(1)} %add_rsqrt_fusion.1) | copy-start | bytes 3076
  9.5 3.5 copy-start.2
  15.6 5.4 copy-start.12
  15.6 5.4 copy-start.8
  15.6 5.4 copy-start.15
  15.6 6.2 copy-start.3
  238.0 492.1 %all-reduce.8.cloned.1.call-start = ((), (), s32[]{:S(2)}) async-start(), calls=%async_computation.1 | async-start | bytes 786432 | tf_op jit(solution)/shard_map/psum | solution.py:141
  412.7 7.2 copy-start.4
  426.3 3.2 copy-start.5
  429.4 7.1 copy-start.4
  443.0 4.1 copy-start.5
  447.1 7.1 copy-start.4
  460.7 4.1 copy-start.5
  464.8 7.1 copy-start.4
  478.4 4.1 copy-start.5
  482.5 7.1 copy-start.4
  496.1 4.1 copy-start.5
  500.2 7.1 copy-start.4
  513.8 4.1 copy-start.5
  517.9 7.1 copy-start.4
  531.5 4.1 copy-start.5
  535.6 7.1 copy-start.4
  549.2 4.1 copy-start.5
  553.3 180.5 %copy-start.9 = (bf16[256,512]{1,0:T(8,128)(2,1)S(1)}, bf16[256,512]{1,0:T(8,128)(2,1)}, u32[]{:S(2)}) copy-start(bf16[256,512]{1,0:T(8,128)(2,1)} %param.16) | copy-start | bytes 786436
  553.3 180.5 %copy-start.19 = (f32[256]{0:T(256)S(1)}, f32[256]{0:T(256)}, u32[]{:S(2)}) copy-start(f32[256]{0:T(256)} %copy-done.18) | copy-start | bytes 3076
  553.3 180.5 %copy-start.21 = (f32[256]{0:T(256)S(1)}, f32[256]{0:T(256)}, u32[]{:S(2)}) copy-start(f32[256]{0:T(256)} %copy-done.20) | copy-start | bytes 3076
  553.3 225.9 %all-reduce.10.cloned.1.call-start = ((), (), s32[]{:S(2)}) async-start(), calls=%async_computation.2 | async-start | bytes 1048576 | tf_op jit(solution)/shard_map/psum | solution.py:95
  730.1 54.1 %copy-start.14 = (f32[256,128]{1,0:T(8,128)S(1)}, f32[256,128]{1,0:T(8,128)}, u32[]{:S(2)}) copy-start(f32[256,128]{1,0:T(8,128)} %get-tuple-element.638) | copy-start | bytes 393220
  732.0 52.8 %copy-start.13 = (f32[256,128]{1,0:T(8,128)S(1)}, f32[256,128]{1,0:T(8,128)}, u32[]{:S(2)}) copy-start(f32[256,128]{1,0:T(8,128)} %get-tuple-element.639) | copy-start | bytes 393220
  (56 other events, 92.0 us)
Sparse Core Ops, SparseCore 0:
  238.1 172.3 all-reduce.5
  553.5 176.5 all-reduce.7
  733.2 46.0 all-reduce.9
where the time goes:
time: 798 us; the launch traced here: 792 us
  waiting for transfers between devices  262 us (33%)
  blocking collectives  257 us (32%)
  matrix products  165 us (21%)
  other arithmetic  53 us (7%)
  local copies, waits for them, and re-layouts  28.9 us (4%)
  between operations  14 us (2%)
  loops' own time  12.3 us (2%)
    psum x1, waiting for transfers between devices, shards(): query_gradient, d_wk, d_wv = lax.psum((query_gradient, d_wk, d_wv), 'tok')  175 us
    psum x1, blocking collectives, shards(): lax.psum((total * factor, accum * spread(factor, head_size)), 'tok')  128 us
    pmax x1, blocking collectives, shards(): global_max = lax.pmax(row_max, 'tok')  128 us
    psum x1, waiting for transfers between devices, shards(): lax.psum((total * factor, accum * spread(factor, head_size)), 'tok')  44 us
    psum x1, waiting for transfers between devices, shards(): lax.psum(jnp.dot(attn, w_out, preferred_element_type=f32).astype(jnp.bflo...  43.4 us
    dot_general x16, matrix products, tile(): cross = jnp.dot(anchors.T, points, precision=lax.Precision.HIGHEST)  28.9 us
    dot_general x16, matrix products, tile(): jnp.dot(tok_block, w_value, preferred_element_type=f32).astype(bf16)  22 us
    dot_general x16, matrix products, tile(): jnp.dot(tok_block, w_key, preferred_element_type=f32).astype(bf16)  21.9 us
  transfers between devices with their start and end apart: 3, of which 3 were waited for; matrix products, arithmetic and copies ran while one was open for 1% of the time, Pallas kernels for 0%

commit v1 on v0

v1 whole, which is shorter than its diff:
```python
import functools

import jax
import jax.numpy as jnp
from jax import lax
from jax.experimental import pallas as pl
from jax.experimental.pallas import tpu as pltpu
from jax.sharding import Mesh, PartitionSpec as P

f32 = jnp.float32
bf16 = jnp.bfloat16
HS = 64
STAT = 128
Z_MIN = 1e-25
VMEM = 56 * 1024 * 1024
NT = (((1,), (1,)), ((), ()))
TN = (((0,), (0,)), ((), ()))


def nn(a, b):
    return jnp.dot(a, b, preferred_element_type=f32)


def nt(a, b):
    return lax.dot_general(a, b, NT, preferred_element_type=f32)


def tn(a, b):
    return lax.dot_general(a, b, TN, preferred_element_type=f32)


def iota(shape, dim):
    return lax.broadcasted_iota(jnp.int32, shape, dim)


def one_hot(hit):
    return jnp.where(hit, 1.0, 0.0).astype(bf16)


def norm_rows(v):
    mean=jnp.mean(v,axis=-1,keepdims=True)
    d=v-mean
    var=jnp.mean(d*d,axis=-1,keepdims=True)
    return d*lax.rsqrt(var+1e-5)

def column(row, n):
    r=lax.broadcasted_iota(jnp.int32,(n,n),0); c=lax.broadcasted_iota(jnp.int32,(n,n),1)
    return jnp.sum(jnp.where(r==c,jnp.broadcast_to(row,(n,n)),0.0),axis=1,keepdims=True)

def main_kernel(lat, heads, tb, rc, tc, where_ref, gamma_ref, tok_ref, pts_ref, lat_ref, anc_ref, wq_ref, wk_ref, wv_ref, wo_ref, du_ref,
                send_ref, keep_ref, latn_out, q_out, do_out, r_out,
                p_s, r_s, shift_s, anch_s, x_s, eh_s, acc_s, z_s):
    step=pl.program_id(0); steps=pl.num_programs(0)
    width=heads*HS
    rows=heads*lat
    feat=tok_ref.shape[1]
    lane=lax.broadcasted_iota(jnp.int32,(lat,width),1)

    @pl.when(step==0)
    def _():
        latn=norm_rows(lat_ref[...].astype(f32)).astype(bf16)
        latn_out[...]=latn
        q=(nn(latn,wq_ref[...])*(HS**-0.5)).astype(bf16)
        do=nt(du_ref[...],wo_ref[...]).astype(bf16)
        q_out[...]=q; do_out[...]=do
        for k in range(3):
            col=column(anc_ref[k:k+1,:],lat)
            anch_s[k]=jnp.broadcast_to(col,(lat,128))
        box=jnp.zeros((lat,1),f32)
        for k in range(3):
            a=anch_s[k][:,0:1]
            lo=jnp.min(pts_ref[k:k+1,:],axis=1,keepdims=True); hi=jnp.max(pts_ref[k:k+1,:],axis=1,keepdims=True)
            gap=jnp.maximum(jnp.maximum(lo-a,a-hi),0.0)
            box=box+gap*gap
        for h in range(heads):
            mask=(lane>=h*HS)&(lane<(h+1)*HS)
            zero=jnp.zeros((),bf16)
            p=nt(jnp.where(mask,q,zero),wk_ref[...]).astype(bf16)
            r=nt(jnp.where(mask,do,zero),wv_ref[...]).astype(bf16)
            p_s[h*lat:(h+1)*lat,:]=p
            r_s[h*lat:(h+1)*lat,:]=r
            r_out[h*lat:(h+1)*lat,:]=r
            pf=p.astype(f32)
            bound=jnp.sqrt(jnp.sum(pf*pf,axis=1,keepdims=True))*(feat**0.5)-gamma_ref[h]*box
            hi=bound.astype(bf16).astype(f32)
            lo=(bound-hi).astype(bf16).astype(f32)
            shift_s[h*lat:(h+1)*lat,:]=jnp.broadcast_to(hi+lo,(lat,128))
        acc_s[...]=jnp.zeros_like(acc_s)
        z_s[...]=jnp.zeros_like(z_s)

    def rep(a,n): return jnp.concatenate([a]*(n//128),axis=1) if n>128 else a

    def scores(x,pts,h,r0):
        s=nt(p_s[h*lat+r0:h*lat+r0+rc,:],x)
        return s

    def distance(pts,r0,n):
        d=None
        for k in range(3):
            t=rep(anch_s[k,r0:r0+rc,:],n)-pts[k:k+1,:]
            d=t*t if d is None else d+t*t
        return d

    def add_block(start,x,pts):
        for t0 in range(0,tb,tc):
            xt=x[t0:t0+tc,:]
            pt=pts[:,t0:t0+tc]
            for r0 in range(0,lat,rc):
                d=distance(pt,r0,tc)
                for h in range(heads):
                    a=h*lat+r0
                    s=scores(xt,pt,h,r0)
                    g=nt(r_s[a:a+rc,:],xt)
                    e=jnp.exp(s-(gamma_ref[h]*d+rep(shift_s[a:a+rc,:],tc))).astype(bf16)
                    ef=e.astype(f32)
                    part=ef[:,0:128]
                    for j in range(128,tc,128): part=part+ef[:,j:j+128]
                    z_s[a:a+rc,:]+=part
                    eh_s[a:a+rc,t0:t0+tc]=e
                    eh_s[rows+a:rows+a+rc,t0:t0+tc]=(ef*g).astype(bf16)
        acc_s[...]+=nn(eh_s[...],x)

    start=pl.multiple_of(step*tb,tb)
    x=norm_rows(tok_ref[...].astype(f32)).astype(bf16)
    x_s[pl.ds(start,tb),:]=x
    add_block(start,x,pts_ref[:,pl.ds(start,tb)])

    @pl.when(step==steps-1)
    def _():
        low=jnp.min(jnp.sum(z_s[...],axis=1,keepdims=True))

        @pl.when(jnp.logical_not(low>=Z_MIN))
        def _():
            shift_s[...]=jnp.full_like(shift_s,-jnp.inf)
            def top(i,carry):
                at=pl.multiple_of(i*tb,tb)
                xb=x_s[pl.ds(at,tb),:]; pb=pts_ref[:,pl.ds(at,tb)]
                for t0 in range(0,tb,tc):
                    for r0 in range(0,lat,rc):
                        d=distance(pb[:,t0:t0+tc],r0,tc)
                        for h in range(heads):
                            a=h*lat+r0
                            s=scores(xb[t0:t0+tc,:],None,h,r0)-gamma_ref[h]*d
                            shift_s[a:a+rc,:]=jnp.maximum(shift_s[a:a+rc,:],jnp.broadcast_to(jnp.max(s,axis=1,keepdims=True),(rc,128)))
                return carry
            lax.fori_loop(0,steps,top,0)
            m=shift_s[...]
            hi=m.astype(bf16).astype(f32)
            shift_s[...]=hi+(m-hi).astype(bf16).astype(f32)
            acc_s[...]=jnp.zeros_like(acc_s)
            z_s[...]=jnp.zeros_like(z_s)
            def again(i,carry):
                at=pl.multiple_of(i*tb,tb)
                add_block(at,x_s[pl.ds(at,tb),:],pts_ref[:,pl.ds(at,tb)])
                return carry
            lax.fori_loop(0,steps,again,0)

        z=jnp.sum(z_s[...],axis=1,keepdims=True)
        shift=shift_s[...]
        stat=write_stat(z,shift[:,0:1])
        full=jnp.concatenate([acc_s[0:rows,:].astype(bf16),acc_s[rows:2*rows,:].astype(bf16),stat],axis=1)
        core=where_ref[0]
        half=rows//2; each=lat//2
        for out,c in ((send_ref,1-core),(keep_ref,core)):
            ro=lax.broadcasted_iota(jnp.int32,(half,rows),0); co=lax.broadcasted_iota(jnp.int32,(half,rows),1)
            src=((ro>>2)&1)*lat+c*each+((ro>>3)<<2)+(ro&3)
            pick=jnp.where(co==src,1.0,0.0).astype(bf16)
            out[...]=nn(pick,full).astype(bf16)

def main_call(where,gamma,tokens,coords,latents,anchors,wq,wk,wv,wo,du,tb=2048,rc=256,tc=512):
    toks,feat=tokens.shape; lat,dl=latents.shape; heads=gamma.shape[0]; width=heads*HS; rows=heads*lat
    steps=toks//tb
    cols=2*feat+128
    full=lambda a: pl.BlockSpec(a.shape,lambda i:(0,)*a.ndim)
    smem=pl.BlockSpec(memory_space=pltpu.SMEM)
    outs=[jax.ShapeDtypeStruct((rows//2,cols),bf16)]*2+[jax.ShapeDtypeStruct((lat,dl),bf16),jax.ShapeDtypeStruct((lat,width),bf16),jax.ShapeDtypeStruct((lat,width),bf16),jax.ShapeDtypeStruct((rows,feat),bf16)]
    return pl.pallas_call(
        functools.partial(main_kernel,lat,heads,tb,rc,tc),
        grid=(steps,),
        out_shape=outs,
        in_specs=[smem,smem,pl.BlockSpec((tb,feat),lambda i:(i,0))]+[full(a) for a in (coords,latents,anchors,wq,wk,wv,wo,du)],
        out_specs=[full(o) for o in outs],
        scratch_shapes=[pltpu.VMEM((rows,feat),bf16),pltpu.VMEM((rows,feat),bf16),pltpu.VMEM((rows,128),f32),pltpu.VMEM((3,lat,128),f32),
            pltpu.VMEM((toks,feat),bf16),pltpu.VMEM((2*rows,tb),bf16),pltpu.VMEM((2*rows,feat),f32),pltpu.VMEM((rows,128),f32)],
        compiler_params=pltpu.CompilerParams(vmem_limit_bytes=VMEM),
        name="token_pass",
    )(where,gamma,tokens,coords,latents,anchors,wq,wk,wv,wo,du)


def read_stat(stat):
    return stat[:, 0:1] + stat[:, 1:2], stat[:, 2:3] + stat[:, 3:4]


def write_stat(z, shift):
    rows = z.shape[0]
    at = iota((rows, STAT), 1)
    z_hi = z.astype(bf16).astype(f32)
    s_hi = shift.astype(bf16).astype(f32)
    stat = jnp.where(at == 2, s_hi, jnp.where(at == 3, shift - s_hi, 0.0))
    stat = jnp.where(at == 0, z_hi, jnp.where(at == 1, z - z_hi, stat))
    return stat.astype(bf16)


def pair_kernel(a_ref, b_ref, out_ref):
    wide = a_ref.shape[1] - STAT
    za, sa = read_stat(a_ref[:, wide:].astype(f32))
    zb, sb = read_stat(b_ref[:, wide:].astype(f32))
    shift = jnp.maximum(sa, sb)
    wa = jnp.exp(sa - shift)
    wb = jnp.exp(sb - shift)
    out_ref[:, 0:wide] = (a_ref[:, 0:wide].astype(f32) * wa + b_ref[:, 0:wide].astype(f32) * wb).astype(bf16)
    out_ref[:, wide:] = write_stat(za * wa + zb * wb, shift)


def owner_kernel(lat, heads, chips, where_ref, all_ref, r_ref, wk_ref, wv_ref, wo_ref, wq_ref, fg_out, part_out):
    rows = all_ref.shape[0] // chips
    per = rows // heads
    feat = wk_ref.shape[0]
    width = wk_ref.shape[1]
    wide = 2 * feat
    group = where_ref[0] * chips + where_ref[1]
    z, shift = read_stat(all_ref[:, wide:].astype(f32))
    z = z.reshape(chips, rows, 1)
    shift = shift.reshape(chips, rows, 1)
    top = jnp.max(shift, axis=0, keepdims=True)
    w = jnp.exp(shift - top)
    total = jnp.sum(z * w, axis=0)
    sums = jnp.sum(all_ref[:, 0:wide].astype(f32).reshape(chips, rows, wide) * w, axis=0)
    inv = 1.0 / total
    f = sums[:, 0:feat] * inv
    at = iota((rows, heads * lat), 0)
    src = (at // per) * lat + group * per + at % per
    r = nn(one_hot(iota((rows, heads * lat), 1) == src), r_ref[...])
    delta = jnp.sum(f * r, axis=1, keepdims=True)
    g = sums[:, feat:wide] * inv - delta * f
    fb = f.astype(bf16)
    gb = g.astype(bf16)
    fg_out[...] = jnp.concatenate([fb, gb], axis=1)
    mine = iota((rows, width), 1) // HS == iota((rows, width), 0) // per
    o = jnp.where(mine, nn(fb, wv_ref[...]), 0.0).astype(bf16)
    dq = jnp.where(mine, nn(gb, wk_ref[...]) * (HS ** -0.5), 0.0).astype(bf16)
    up = nn(o, wo_ref[...])
    dn = nt(dq, wq_ref[...])
    up = up + pltpu.roll(up, per, 0)
    dn = dn + pltpu.roll(dn, per, 0)
    part_out[...] = jnp.where(iota(up.shape, 0) < per, up, dn).astype(bf16)


def spread_kernel(chips, heads, groups, where_ref, *refs):
    parts, (fg_ref, lat_ref, out_ref) = refs[:groups], refs[groups:]
    rows = fg_ref.shape[0]
    per = rows // heads
    lat = lat_ref.shape[0]
    group = where_ref[0] * chips + where_ref[1]
    tot = parts[0][...].astype(f32)
    for p in parts[1:]:
        tot = tot + p[...].astype(f32)
    at = iota((rows, lat), 0)
    x = nn(one_hot(iota((rows, lat), 1) == group * per + at % per), lat_ref[...])
    mean = jnp.mean(x, axis=-1, keepdims=True)
    d = x - mean
    inv = lax.rsqrt(jnp.mean(d * d, axis=-1, keepdims=True) + 1e-5)
    xhat = d * inv
    back = inv * (tot - jnp.mean(tot, axis=-1, keepdims=True) - xhat * jnp.mean(tot * xhat, axis=-1, keepdims=True))
    ud = jnp.where(iota(tot.shape, 0) < per, tot, back)
    row = jnp.concatenate([fg_ref[...].astype(f32), ud], axis=1)
    block = jnp.concatenate([row, row], axis=0).astype(bf16)
    for s in range(chips // 2):
        out_ref[s * 2 * rows:(s + 1) * 2 * rows, :] = block


def finish_kernel(chips, heads, where_ref, own_ref, other_ref, q_ref, do_ref, latn_ref, wk_ref, wv_ref, du_ref,
                  up_out, dl_out, dwq_out, dwk_out, dwv_out, dwo_out):
    lat, width = q_ref.shape
    feat = wk_ref.shape[0]
    half = own_ref.shape[0]
    rows = half // chips
    per = rows // heads
    core = where_ref[0]

    def place(at):
        c = jnp.where(at < half, core, 1 - core)
        chip = (at % half) // rows
        return (c * chips + chip) * per + at % per, (at % rows) // per

    both = jnp.concatenate([own_ref[...], other_ref[...]], axis=0)
    f = both[:, 0:feat]
    g = both[:, feat:2 * feat]
    ud = both[:, 2 * feat:]
    l, _ = place(iota((2 * half, lat), 0))
    spread = one_hot(l == iota((2 * half, lat), 1))
    _, h = place(iota((2 * half, width), 0))
    mine = h == iota((2 * half, width), 1) // HS
    zero = jnp.zeros((), f32)
    do = jnp.where(mine, nn(spread, do_ref[...]), zero).astype(bf16)
    q = jnp.where(mine, nn(spread, q_ref[...]), zero).astype(bf16)
    dwv_out[...] = tn(f, do)
    dwk_out[...] = tn(g, q)
    o = jnp.where(mine, nn(f, wv_ref[...]), zero).astype(bf16)
    dq = jnp.where(mine, nn(g, wk_ref[...]) * (HS ** -0.5), zero).astype(bf16)
    l, h = place(iota((lat, 2 * half), 1))
    hit = l == iota((lat, 2 * half), 0)
    gather = one_hot(hit)
    o = nn(gather, o).astype(bf16)
    dq = nn(gather, dq).astype(bf16)
    dwo_out[...] = tn(o, du_ref[...])
    dwq_out[...] = tn(latn_ref[...], dq)
    up_out[...] = nn(one_hot(hit & (h == 0)), ud).astype(bf16)
    dl_out[...] = nn(one_hot(hit & (h == 1)), ud)


def small(kernel, outs, smem, name):
    one = pl.BlockSpec(memory_space=pltpu.VMEM)
    params = pltpu.CompilerParams(vmem_limit_bytes=VMEM)
    shapes = [jax.ShapeDtypeStruct(s, t) for s, t in outs]

    def call(*args):
        specs = [pl.BlockSpec(memory_space=pltpu.SMEM)] * smem + [one] * (len(args) - smem)
        return pl.pallas_call(
            kernel, out_shape=shapes, in_specs=specs, out_specs=[one] * len(shapes), compiler_params=params, name=name
        )(*args)

    return call


def shards(tokens, coords, latents, anchors, gamma, w_query, w_key, w_value, w_out, d_update):
    lat, dl = latents.shape
    feat = tokens.shape[1]
    heads = gamma.shape[0]
    width = heads * HS
    chips = lax.axis_size("chip")
    groups = lax.axis_size("head")
    half = heads * lat // 2
    rows = half // chips
    wide = 2 * feat
    where = jnp.stack([lax.axis_index("core"), lax.axis_index("chip")]).astype(jnp.int32)
    swap = [(0, 1), (1, 0)]

    send, keep, latn, q, do, r = main_call(
        where, gamma, tokens, coords, latents, anchors, w_query, w_key, w_value, w_out, d_update
    )
    got = lax.ppermute(send, "core", swap)
    (pair,) = small(pair_kernel, [((half, wide + STAT), bf16)], 0, "pair_sum")(keep, got)
    shares = lax.all_to_all(pair.reshape(chips, rows, wide + STAT), "chip", 0, 0, tiled=True)
    fg, part = small(
        functools.partial(owner_kernel, lat, heads, chips), [((rows, wide), bf16), ((rows, dl), bf16)], 1, "owner_rows"
    )(where, shares.reshape(half, wide + STAT), r, w_key, w_value, w_out, w_query)
    parts = [part]
    for k in range(1, groups):
        parts.append(lax.ppermute(part, "head", [(i, (i + k) % groups) for i in range(groups)]))
    (copies,) = small(
        functools.partial(spread_kernel, chips, heads, groups), [((half, wide + dl), bf16)], 1, "spread_rows"
    )(where, *parts, fg, latents)
    own = lax.all_to_all(copies.reshape(chips, rows, wide + dl), "chip", 0, 0, tiled=True).reshape(half, wide + dl)
    other = lax.ppermute(own, "core", swap)
    outs = [((lat, dl), bf16), ((lat, dl), f32), ((dl, width), f32), ((feat, width), f32), ((feat, width), f32), ((width, dl), f32)]
    return tuple(
        small(functools.partial(finish_kernel, chips, heads), outs, 1, "finish")(
            where, own, other, q, do, latn, w_key, w_value, d_update
        )
    )


def solution(mesh):
    toks, head = mesh.devices.shape
    fine = Mesh(mesh.devices.reshape(toks // 2, 2, head), ("chip", "core", "head"))
    tok = ("chip", "core")
    return jax.shard_map(
        shards,
        mesh=fine,
        in_specs=(
            P(tok, None),
            P(None, tok),
            P(),
            P(),
            P("head"),
            P(None, "head"),
            P(None, "head"),
            P(None, "head"),
            P("head", None),
            P(),
        ),
        out_specs=(P(), P(), P(None, "head"), P(None, "head"), P(None, "head"), P("head", None)),
        check_vma=False,
    )
```

time: 798 us -> 94.7 us (0.12)
  waiting for transfers between devices: 262 us -> 6.32 us
  blocking collectives: 257 us -> 40.5 us
  matrix products: 165 us -> 0 us
  other arithmetic: 53 us -> 0.67 us
  Pallas kernels: 0 us -> 31.6 us
  local copies, waits for them, and re-layouts: 28.9 us -> 2.12 us
  between operations: 14 us -> 0.65 us
  loops' own time: 12.3 us -> 0 us
  starting transfers between devices: 0.12 us -> 12.4 us
    psum x3 -> x0, waiting for transfers between devices: 262 us -> none  [the longest x1 175 us: shards(): query_gradient, d_wk, d_wv = lax.psum((query_gradient, d_wk, d_wv), 'tok')]
    dot_general x126 -> x0, matrix products: 165 us -> none  [the longest x16 28.9 us: tile(): cross = jnp.dot(anchors.T, points, precision=lax.Precision.HIGHEST)]
    psum x1 -> x0, blocking collectives: 128 us -> none  [shards(): lax.psum((total * factor, accum * spread(factor, head_size)), 'tok')]
    pmax x1 -> x0, blocking collectives: 128 us -> none  [shards(): global_max = lax.pmax(row_max, 'tok')]
    all_to_all x0 -> x2, blocking collectives: none -> 40.5 us  [the longest x1 22.3 us: shards(): lax.all_to_all(pair.reshape(chips, rows, wide + STAT), 'chip', 0, 0, tile...]
    pallas_call x0 -> x5, Pallas kernels: none -> 31.6 us  [the longest x1 21 us: main_call(): pl.pallas_call(functools.partial(main_kernel, lat, heads, tb, rc, tc), gr...]
    reduce_sum x30 -> x0, other arithmetic: 31 us -> none  [the longest x16 11.8 us: tile(): jnp.sum(points * points, axis=0)[None, :]]
    dynamic_slice x16 -> x0, local copies, waits for them, and re-layouts: 19.6 us -> none  [shards(): (row_max, total, accum), _ = lax.scan(forward_step, init, steps_all)]
  transfers between devices with their start and end apart: 3 -> 5, of which waited for: 3 -> 4; matrix products, arithmetic and copies ran while one was open for 1% -> 0% of each run, Pallas kernels for 0% -> 0%
where the time goes in v1:
time: 94.7 us; the launch traced here: 94.3 us
  blocking collectives  40.5 us (43%)
  Pallas kernels  31.6 us (33%)
  starting transfers between devices  12.4 us (13%)
  waiting for transfers between devices  6.32 us (7%)
  local copies, waits for them, and re-layouts  2.12 us (2%)
    all_to_all x1, blocking collectives, shards(): lax.all_to_all(pair.reshape(chips, rows, wide + STAT), 'chip', 0, 0, tile...  22.3 us
    pallas_call x1, Pallas kernels, main_call(): pl.pallas_call(functools.partial(main_kernel, lat, heads, tb, rc, tc), gr...  21 us
    all_to_all x1, blocking collectives, shards(): lax.all_to_all(copies.reshape(chips, rows, wide + dl), 'chip', 0, 0, tile...  18.2 us
    pallas_call x4, Pallas kernels, call(): pl.pallas_call(kernel, out_shape=shapes, in_specs=specs, out_specs=[one]...  10.7 us
    ppermute x1, starting transfers between devices, shards(): other = lax.ppermute(own, 'core', swap)  5.56 us
    ppermute x3, starting transfers between devices, shards(): lax.ppermute(part, 'head', [(i, (i + k) % groups) for i in range(groups)])  3.59 us
    ppermute x3, waiting for transfers between devices, shards(): lax.ppermute(part, 'head', [(i, (i + k) % groups) for i in range(groups)])  3.31 us
    ppermute x1, starting transfers between devices, shards(): got = lax.ppermute(send, 'core', swap)  3.26 us
  transfers between devices with their start and end apart: 5, of which 4 were waited for; matrix products, arithmetic and copies ran while one was open for 0% of the time, Pallas kernels for 0%

profile of v1, /device:TPU:1, one launch (start us, length us, event | category | flops | bytes accessed | tf_op | source)
XLA Modules:
  0.0 94.3 jit_solution(2949030186384576944)
XLA Ops:
  0.6 0.7 pad_add_fusion.where_ref
  1.3 21.0 %token_pass.1 = (bf16[256,640]{1,0:T(8,128)(2,1)}, bf16[256,640]{1,0:T(8,128)(2,1)}, bf16[256,512]{1,0:T(8,128)(2,1)}, bf16[256,128]{1,0:T(8,128)(2,1)}, bf16[25...) custom-call(s32[2]{0:T(128)} %pad_add_fusion.where_ref, f32[2]{0:T(128)} %gamma_ref.1, bf16[8192,256]{1,0:T(8,128)(2,1)} %tok_ref.1, ...), custom_call_target="tpu_custom_call" | custom-call | tf_op jit(solution)/shard_map/token_pass/pallas_call | solution.py:177
  22.3 3.3 %collective-permute-start = (bf16[256,640]{1,0:T(8,128)(2,1)}, bf16[256,640]{1,0:T(8,128)(2,1)S(1)}, u32[]{:S(2)}, u32[]{:S(2)}) collective-permute-start(bf16[256,640]{1,0:T(8,128)(2,1)} %get-tuple-element.15), channel_id=1, source_target_pairs={{0,4},{4,0},{1,5},{5,1},{2,6},{6,2},{3,7},{7,3},{8,12},{12,8},{9,1... | collective-permute-start | bytes 983048 | tf_op jit(solution)/shard_map/ppermute | solution.py:342
  25.5 1.5 %collective-permute-done.b_ref = bf16[256,640]{1,0:T(8,128)(2,1)S(1)} collective-permute-done((bf16[256,640]{1,0:T(8,128)(2,1)}, bf16[256,640]{1,0:T(8,128)(2,1)S(1)}, u32[]{:S(2)}, u32[]{:S(2)}) %collective-permute-start) | collective-permute-done | bytes 327712 | tf_op jit(solution)/shard_map/ppermute | solution.py:342
  27.0 0.0 copy-start.2
  27.0 0.7 copy-done.2
  27.7 2.2 %pair_sum.1 = bf16[256,640]{1,0:T(8,128)(2,1)} custom-call(bf16[256,640]{1,0:T(8,128)(2,1)} %get-tuple-element.14.a_ref, bf16[256,640]{1,0:T(8,128)(2,1)} %copy-done.2), custom_call_target="tpu_custom_call" | custom-call | tf_op jit(solution)/shard_map/pair_sum/pallas_call | solution.py:319
  29.9 22.3 %all_to_all.10 = bf16[32,8,640]{2,1,0:T(8,128)(2,1)} all-to-all(bf16[32,8,640]{2,1,0:T(8,128)(2,1)} %bitcast.10), channel_id=1, replica_groups=mesh['chip'=32,'core'=2,'head'=4] {'chip'}, dimensions={0} | all-to-all | bytes 655360 | tf_op jit(solution)/shard_map/all_to_all | solution.py:344
  52.3 2.4 %owner_rows.1 = (bf16[8,512]{1,0:T(8,128)(2,1)}, bf16[8,512]{1,0:T(8,128)(2,1)}) custom-call(s32[2]{0:T(128)} %pad_add_fusion.where_ref, bf16[256,640]{1,0:T(8,128)(2,1)} %bitcast.9, bf16[512,256]{1,0:T(8,128)(2,1)} %get-tuple-element.16.r_ref, bf16[256,128]{1,0:T(8,128)(2,1)} %wk_ref.5, bf16[256,128]{1,0:T(8,128)(2,1)} %wv_ref.5, bf16[128,512]{1,0:T(8,128)(2,1)} %wo_ref.3, ...), custom_call_target="tpu_custom_call" | custom-call | tf_op jit(solution)/shard_map/owner_rows/pallas_call | solution.py:319
  54.7 2.5 %collective-permute-start.3 = (bf16[8,512]{1,0:T(8,128)(2,1)}, bf16[8,512]{1,0:T(8,128)(2,1)S(1)}, u32[]{:S(2)}, u32[]{:S(2)}) collective-permute-start(bf16[8,512]{1,0:T(8,128)(2,1)} %get-tuple-element.17.refs_0_), channel_id=1, source_target_pairs={{0,3},{1,0},{2,1},{3,2},{4,7},{5,4},{6,5},{7,6},{8,11},{9,8},{10,9... | collective-permute-start | bytes 24584 | tf_op jit(solution)/shard_map/ppermute | solution.py:350
  57.1 0.5 collective-permute-start.2
  57.6 0.6 collective-permute-start.1
  58.2 0.0 collective-permute-done.3.refs_3_
  58.2 0.0 copy-start.3
  58.2 3.1 %collective-permute-done.2.refs_2_ = bf16[8,512]{1,0:T(8,128)(2,1)S(1)} collective-permute-done((bf16[8,512]{1,0:T(8,128)(2,1)}, bf16[8,512]{1,0:T(8,128)(2,1)S(1)}, u32[]{:S(2)}, u32[]{:S(2)}) %collective-permute-start.2) | collective-permute-done | bytes 8224 | tf_op jit(solution)/shard_map/ppermute | solution.py:350
  61.3 0.0 copy-start.4
  61.3 0.2 collective-permute-done.1.refs_1_
  61.6 0.0 copy-start.5
  61.6 0.0 copy-done.3
  61.6 0.4 copy-done.4
  61.9 0.2 copy-done.5
  62.2 2.3 %spread_rows.1 = bf16[256,1024]{1,0:T(8,128)(2,1)} custom-call(s32[2]{0:T(128)} %pad_add_fusion.where_ref, bf16[8,512]{1,0:T(8,128)(2,1)} %get-tuple-element.17.refs_0_, bf16[8,512]{1,0:T(8,128)(2,1)} %copy-done.5, bf16[8,512]{1,0:T(8,128)(2,1)} %copy-done.4, bf16[8,512]{1,0:T(8,128)(2,1)} %copy-done.3, bf16[8,512]{1,0:T(8,128)(2,1)} %get-tuple-element.18.refs_4_, ...), custom_call_target="tpu_custom_call" | custom-call | tf_op jit(solution)/shard_map/spread_rows/pallas_call | solution.py:319
  64.4 18.2 %all_to_all.11 = bf16[32,8,1024]{2,1,0:T(8,128)(2,1)S(1)} all-to-all(bf16[32,8,1024]{2,1,0:T(8,128)(2,1)} %bitcast.6), channel_id=1, replica_groups=mesh['chip'=32,'core'=2,'head'=4] {'chip'}, dimensions={0} | all-to-all | bytes 1048576 | tf_op jit(solution)/shard_map/all_to_all | solution.py:354
  82.6 0.0 copy-start
  82.6 5.6 %collective-permute-start.4 = (bf16[256,1024]{1,0:T(8,128)(2,1)S(1)}, bf16[256,1024]{1,0:T(8,128)(2,1)S(1)}, u32[]{:S(2)}, u32[]{:S(2)}) collective-permute-start(bf16[256,1024]{1,0:T(8,128)(2,1)S(1)} %bitcast.7), channel_id=1, source_target_pairs={{0,4},{4,0},{1,5},{5,1},{2,6},{6,2},{3,7},{7,3},{8,12},{12,8},{9,1... | collective-permute-start | bytes 1572872 | tf_op jit(solution)/shard_map/ppermute | solution.py:355
  88.2 1.5 %collective-permute-done.4.other_ref = bf16[256,1024]{1,0:T(8,128)(2,1)S(1)} collective-permute-done((bf16[256,1024]{1,0:T(8,128)(2,1)S(1)}, bf16[256,1024]{1,0:T(8,128)(2,1)S(1)}, u32[]{:S(2)}, u32[]{:S(2)}) %collective-permute-start.4) | collective-permute-done | bytes 524320 | tf_op jit(solution)/shard_map/ppermute | solution.py:355
  89.7 0.0 copy-start.1
  89.7 0.0 copy-done
  89.7 0.8 copy-done.1
  90.5 3.8 %finish.1 = (bf16[256,512]{1,0:T(8,128)(2,1)}, f32[256,512]{1,0:T(8,128)}, f32[512,128]{1,0:T(8,128)}, f32[256,128]{1,0:T(8,128)}, f32[256,128]{1,0:T(8,128)}, /*index=5*/f32[128,512]{1,0:T(8,128)}) custom-call(s32[2]{0:T(128)} %pad_add_fusion.where_ref, bf16[256,1024]{1,0:T(8,128)(2,1)} %bitcast.8, bf16[256,1024]{1,0:T(8,128)(2,1)} %copy-done.1, ...), custom_call_target="tpu_custom_call" | custom-call | tf_op jit(solution)/shard_map/finish/pallas_call | solution.py:319
Async XLA Ops:
  22.3 4.7 %collective-permute-start = (bf16[256,640]{1,0:T(8,128)(2,1)}, bf16[256,640]{1,0:T(8,128)(2,1)S(1)}, u32[]{:S(2)}, u32[]{:S(2)}) collective-permute-start(bf16[256,640]{1,0:T(8,128)(2,1)} %get-tuple-element.15), channel_id=1, source_target_pairs={{0,4},{4,0},{1,5},{5,1},{2,6},{6,2},{3,7},{7,3},{8,12},{12,8},{9,1... | collective-permute-start | bytes 983048 | tf_op jit(solution)/shard_map/ppermute | solution.py:342
  27.0 0.7 copy-start.2
  54.7 3.6 %collective-permute-start.3 = (bf16[8,512]{1,0:T(8,128)(2,1)}, bf16[8,512]{1,0:T(8,128)(2,1)S(1)}, u32[]{:S(2)}, u32[]{:S(2)}) collective-permute-start(bf16[8,512]{1,0:T(8,128)(2,1)} %get-tuple-element.17.refs_0_), channel_id=1, source_target_pairs={{0,3},{1,0},{2,1},{3,2},{4,7},{5,4},{6,5},{7,6},{8,11},{9,8},{10,9... | collective-permute-start | bytes 24584 | tf_op jit(solution)/shard_map/ppermute | solution.py:350
  57.1 4.2 %collective-permute-start.2 = (bf16[8,512]{1,0:T(8,128)(2,1)}, bf16[8,512]{1,0:T(8,128)(2,1)S(1)}, u32[]{:S(2)}, u32[]{:S(2)}) collective-permute-start(bf16[8,512]{1,0:T(8,128)(2,1)} %get-tuple-element.17.refs_0_), channel_id=1, source_target_pairs={{0,2},{1,3},{2,0},{3,1},{4,6},{5,7},{6,4},{7,5},{8,10},{9,11},{10,... | collective-permute-start | bytes 24584 | tf_op jit(solution)/shard_map/ppermute | solution.py:350
  57.6 3.9 %collective-permute-start.1 = (bf16[8,512]{1,0:T(8,128)(2,1)}, bf16[8,512]{1,0:T(8,128)(2,1)S(1)}, u32[]{:S(2)}, u32[]{:S(2)}) collective-permute-start(bf16[8,512]{1,0:T(8,128)(2,1)} %get-tuple-element.17.refs_0_), channel_id=1, source_target_pairs={{0,1},{1,2},{2,3},{3,0},{4,5},{5,6},{6,7},{7,4},{8,9},{9,10},{10,1... | collective-permute-start | bytes 24584 | tf_op jit(solution)/shard_map/ppermute | solution.py:350
  58.2 3.3 %copy-start.3 = (bf16[8,512]{1,0:T(8,128)(2,1)}, bf16[8,512]{1,0:T(8,128)(2,1)S(1)}, u32[]{:S(2)}) copy-start(bf16[8,512]{1,0:T(8,128)(2,1)S(1)} %collective-permute-done.3.refs_3_) | copy-start | bytes 24580
  61.3 0.6 copy-start.4
  61.6 0.6 copy-start.5
  82.6 7.1 %copy-start = (bf16[32,8,1024]{2,1,0:T(8,128)(2,1)}, bf16[32,8,1024]{2,1,0:T(8,128)(2,1)S(1)}, u32[]{:S(2)}) copy-start(bf16[32,8,1024]{2,1,0:T(8,128)(2,1)S(1)} %all_to_all.11) | copy-start | bytes 1572868
  82.6 7.1 %collective-permute-start.4 = (bf16[256,1024]{1,0:T(8,128)(2,1)S(1)}, bf16[256,1024]{1,0:T(8,128)(2,1)S(1)}, u32[]{:S(2)}, u32[]{:S(2)}) collective-permute-start(bf16[256,1024]{1,0:T(8,128)(2,1)S(1)} %bitcast.7), channel_id=1, source_target_pairs={{0,4},{4,0},{1,5},{5,1},{2,6},{6,2},{3,7},{7,3},{8,12},{12,8},{9,1... | collective-permute-start | bytes 1572872 | tf_op jit(solution)/shard_map/ppermute | solution.py:355
  89.7 0.8 copy-start.1

commit v2 on v1

v2 whole, which is shorter than its diff:
```python
import functools

import jax
import jax.numpy as jnp
from jax import lax
from jax.experimental import pallas as pl
from jax.experimental.pallas import tpu as pltpu
from jax.sharding import Mesh, PartitionSpec as P

f32 = jnp.float32
bf16 = jnp.bfloat16
HS = 64
STAT = 128
Z_MIN = 1e-25
MAIN_VMEM = 58 * 1024 * 1024
VMEM = 10 * 1024 * 1024
NT = (((1,), (1,)), ((), ()))
TN = (((0,), (0,)), ((), ()))


def nn(a, b):
    return jnp.dot(a, b, preferred_element_type=f32)


def nt(a, b):
    return lax.dot_general(a, b, NT, preferred_element_type=f32)


def tn(a, b):
    return lax.dot_general(a, b, TN, preferred_element_type=f32)


def iota(shape, dim):
    return lax.broadcasted_iota(jnp.int32, shape, dim)


def one_hot(hit):
    return jnp.where(hit, 1.0, 0.0).astype(bf16)


def norm_rows(v):
    mean = jnp.mean(v, axis=-1, keepdims=True)
    d = v - mean
    var = jnp.mean(d * d, axis=-1, keepdims=True)
    return d * lax.rsqrt(var + 1e-5)


def column(row, n):
    return jnp.sum(
        jnp.where(iota((n, n), 0) == iota((n, n), 1), jnp.broadcast_to(row, (n, n)), 0.0), axis=1, keepdims=True
    )


def two_parts(v):
    high = v.astype(bf16).astype(f32)
    return high + (v - high).astype(bf16).astype(f32)


def token_kernel(lat, heads, tb, tc, core_ref, gamma_ref, tok_ref, pts_ref, lat_ref, anc_ref, wq_ref, wk_ref, wv_ref,
                 wo_ref, du_ref, send_ref, keep_ref, latn_out, q_out, do_out, r_out,
                 anc_s, p_s, r_s, shift_s, x_s, acc_s, z_s):
    step = pl.program_id(0)
    steps = pl.num_programs(0)
    rows = heads * lat
    feat = tok_ref.shape[1]

    @pl.when(step == 0)
    def _():
        latn = norm_rows(lat_ref[...].astype(f32)).astype(bf16)
        latn_out[...] = latn
        q = (nn(latn, wq_ref[...]) * (HS ** -0.5)).astype(bf16)
        do = nt(du_ref[...], wo_ref[...]).astype(bf16)
        q_out[...] = q
        do_out[...] = do
        box = jnp.zeros((lat, 1), f32)
        for k in range(3):
            a = column(anc_ref[k:k + 1, :], lat)
            anc_s[k] = jnp.broadcast_to(a, (lat, 128))
            low = jnp.min(pts_ref[k:k + 1, :], axis=1, keepdims=True)
            high = jnp.max(pts_ref[k:k + 1, :], axis=1, keepdims=True)
            gap = jnp.maximum(jnp.maximum(low - a, a - high), 0.0)
            box = box + gap * gap
        for h in range(heads):
            at = slice(h * lat, (h + 1) * lat)
            mine = iota(q.shape, 1) // HS == h
            p = nt(jnp.where(mine, q, jnp.zeros((), bf16)), wk_ref[...]).astype(bf16)
            r = nt(jnp.where(mine, do, jnp.zeros((), bf16)), wv_ref[...]).astype(bf16)
            p_s[at, :] = p
            r_s[at, :] = r
            r_out[at, :] = r
            size = p.astype(f32)
            size = jnp.sqrt(jnp.sum(size * size, axis=1, keepdims=True)) * (feat ** 0.5)
            shift_s[at, :] = jnp.broadcast_to(two_parts(size - gamma_ref[h] * box), (lat, 128))
        acc_s[...] = jnp.zeros_like(acc_s)
        z_s[...] = jnp.zeros_like(z_s)

    def wide(a):
        return jnp.concatenate([a] * (tc // 128), axis=1)

    def scores(x, pts):
        s = nt(p_s[...], x)
        dist = None
        for k in range(3):
            t = wide(anc_s[k]) - pts[k:k + 1, :]
            dist = t * t if dist is None else dist + t * t
        heads_s = []
        for h in range(heads):
            at = slice(h * lat, (h + 1) * lat)
            heads_s.append(s[at] - (gamma_ref[h] * dist + wide(shift_s[at, :])))
        return jnp.concatenate(heads_s, axis=0)

    def add_chunk(x, pts):
        s = scores(x, pts)
        g = nt(r_s[...], x)
        e = jnp.exp(s).astype(bf16)
        ef = e.astype(f32)
        part = ef[:, 0:128]
        for j in range(128, tc, 128):
            part = part + ef[:, j:j + 128]
        z_s[...] += part
        acc_s[...] += nn(jnp.concatenate([e, (ef * g).astype(bf16)], axis=0), x)

    start = pl.multiple_of(step * tb, tb)
    for t in range(0, tb, tc):
        x = norm_rows(tok_ref[t:t + tc, :].astype(f32)).astype(bf16)
        x_s[pl.ds(start + t, tc), :] = x
        add_chunk(x, pts_ref[:, pl.ds(start + t, tc)])

    @pl.when(step == steps - 1)
    def _():
        low = jnp.min(jnp.sum(z_s[...], axis=1, keepdims=True))

        @pl.when(jnp.logical_not(low >= Z_MIN))
        def _():
            chunks = x_s.shape[0] // tc
            shift_s[...] = jnp.zeros_like(shift_s)
            z_s[...] = jnp.full_like(z_s, -jnp.inf)

            def top(i, carry):
                at = pl.multiple_of(i * tc, tc)
                s = scores(x_s[pl.ds(at, tc), :], pts_ref[:, pl.ds(at, tc)])
                for j in range(0, tc, 128):
                    z_s[...] = jnp.maximum(z_s[...], s[:, j:j + 128])
                return carry

            lax.fori_loop(0, chunks, top, 0)
            shift_s[...] = jnp.broadcast_to(two_parts(jnp.max(z_s[...], axis=1, keepdims=True)), shift_s.shape)
            acc_s[...] = jnp.zeros_like(acc_s)
            z_s[...] = jnp.zeros_like(z_s)

            def again(i, carry):
                at = pl.multiple_of(i * tc, tc)
                add_chunk(x_s[pl.ds(at, tc), :], pts_ref[:, pl.ds(at, tc)])
                return carry

            lax.fori_loop(0, chunks, again, 0)

        stat = write_stat(jnp.sum(z_s[...], axis=1, keepdims=True), shift_s[:, 0:1])
        full = jnp.concatenate([acc_s[0:rows, :].astype(bf16), acc_s[rows:2 * rows, :].astype(bf16), stat], axis=1)
        core = core_ref[0]
        half = rows // 2
        per = 4
        at = iota((half, rows), 0)
        for out, c in ((send_ref, 1 - core), (keep_ref, core)):
            src = (at // per % heads) * lat + c * (lat // 2) + at // (per * heads) * per + at % per
            out[...] = nn(one_hot(iota((half, rows), 1) == src), full).astype(bf16)


def token_pass(core, gamma, tokens, coords, latents, anchors, wq, wk, wv, wo, du):
    toks, feat = tokens.shape
    lat, dl = latents.shape
    heads = gamma.shape[0]
    width = heads * HS
    rows = heads * lat
    tb = min(4096, toks)
    tc = min(256, tb)
    cols = 2 * feat + STAT

    def full(a):
        return pl.BlockSpec(a.shape, lambda i: (0,) * len(a.shape))

    smem = pl.BlockSpec(memory_space=pltpu.SMEM)
    shapes = [(rows // 2, cols)] * 2 + [(lat, dl), (lat, width), (lat, width), (rows, feat)]
    outs = [jax.ShapeDtypeStruct(s, bf16) for s in shapes]
    held = (coords, latents, anchors, wq, wk, wv, wo, du)
    return pl.pallas_call(
        functools.partial(token_kernel, lat, heads, tb, tc),
        grid=(toks // tb,),
        out_shape=outs,
        in_specs=[smem, smem, pl.BlockSpec((tb, feat), lambda i: (i, 0))] + [full(a) for a in held],
        out_specs=[full(o) for o in outs],
        scratch_shapes=[
            pltpu.VMEM((3, lat, 128), f32),
            pltpu.VMEM((rows, feat), bf16),
            pltpu.VMEM((rows, feat), bf16),
            pltpu.VMEM((rows, 128), f32),
            pltpu.VMEM((toks, feat), bf16),
            pltpu.VMEM((2 * rows, feat), f32),
            pltpu.VMEM((rows, 128), f32),
        ],
        compiler_params=pltpu.CompilerParams(vmem_limit_bytes=MAIN_VMEM),
        name="token_pass",
    )(core, gamma, tokens, *held)


def read_stat(stat):
    return stat[:, 0:1] + stat[:, 1:2], stat[:, 2:3] + stat[:, 3:4]


def write_stat(z, shift):
    rows = z.shape[0]
    at = iota((rows, STAT), 1)
    z_hi = z.astype(bf16).astype(f32)
    s_hi = shift.astype(bf16).astype(f32)
    stat = jnp.where(at == 2, s_hi, jnp.where(at == 3, shift - s_hi, 0.0))
    stat = jnp.where(at == 0, z_hi, jnp.where(at == 1, z - z_hi, stat))
    return stat.astype(bf16)


def pair_kernel(a_ref, b_ref, out_ref):
    wide = a_ref.shape[1] - STAT
    za, sa = read_stat(a_ref[:, wide:].astype(f32))
    zb, sb = read_stat(b_ref[:, wide:].astype(f32))
    shift = jnp.maximum(sa, sb)
    wa = jnp.exp(sa - shift)
    wb = jnp.exp(sb - shift)
    out_ref[:, 0:wide] = (a_ref[:, 0:wide].astype(f32) * wa + b_ref[:, 0:wide].astype(f32) * wb).astype(bf16)
    out_ref[:, wide:] = write_stat(za * wa + zb * wb, shift)


def owner_kernel(lat, heads, chips, core_ref, chip_ref, all_ref, r_ref, wk_ref, wv_ref, wo_ref, wq_ref, fg_out, part_out):
    rows = all_ref.shape[0] // chips
    per = rows // heads
    feat = wk_ref.shape[0]
    width = wk_ref.shape[1]
    wide = 2 * feat
    group = core_ref[0] * chips + chip_ref[0]
    z, shift = read_stat(all_ref[:, wide:].astype(f32))
    z = z.reshape(chips, rows, 1)
    shift = shift.reshape(chips, rows, 1)
    top = jnp.max(shift, axis=0, keepdims=True)
    w = jnp.exp(shift - top)
    total = jnp.sum(z * w, axis=0)
    sums = jnp.sum(all_ref[:, 0:wide].astype(f32).reshape(chips, rows, wide) * w, axis=0)
    inv = 1.0 / total
    f = sums[:, 0:feat] * inv
    at = iota((rows, heads * lat), 0)
    src = (at // per) * lat + group * per + at % per
    r = nn(one_hot(iota((rows, heads * lat), 1) == src), r_ref[...])
    delta = jnp.sum(f * r, axis=1, keepdims=True)
    g = sums[:, feat:wide] * inv - delta * f
    fb = f.astype(bf16)
    gb = g.astype(bf16)
    fg_out[...] = jnp.concatenate([fb, gb], axis=1)
    mine = iota((rows, width), 1) // HS == iota((rows, width), 0) // per
    o = jnp.where(mine, nn(fb, wv_ref[...]), 0.0).astype(bf16)
    dq = jnp.where(mine, nn(gb, wk_ref[...]) * (HS ** -0.5), 0.0).astype(bf16)
    up = nn(o, wo_ref[...])
    dn = nt(dq, wq_ref[...])
    up = up + pltpu.roll(up, per, 0)
    dn = dn + pltpu.roll(dn, per, 0)
    part_out[...] = jnp.where(iota(up.shape, 0) < per, up, dn).astype(bf16)


def spread_kernel(chips, heads, groups, core_ref, chip_ref, *refs):
    parts, (fg_ref, lat_ref, out_ref) = refs[:groups], refs[groups:]
    rows = fg_ref.shape[0]
    per = rows // heads
    lat = lat_ref.shape[0]
    group = core_ref[0] * chips + chip_ref[0]
    tot = parts[0][...].astype(f32)
    for p in parts[1:]:
        tot = tot + p[...].astype(f32)
    at = iota((rows, lat), 0)
    x = nn(one_hot(iota((rows, lat), 1) == group * per + at % per), lat_ref[...])
    mean = jnp.mean(x, axis=-1, keepdims=True)
    d = x - mean
    inv = lax.rsqrt(jnp.mean(d * d, axis=-1, keepdims=True) + 1e-5)
    xhat = d * inv
    back = inv * (tot - jnp.mean(tot, axis=-1, keepdims=True) - xhat * jnp.mean(tot * xhat, axis=-1, keepdims=True))
    ud = jnp.where(iota(tot.shape, 0) < per, tot, back)
    row = jnp.concatenate([fg_ref[...].astype(f32), ud], axis=1)
    block = jnp.concatenate([row, row], axis=0).astype(bf16)
    for s in range(chips // 2):
        out_ref[s * 2 * rows:(s + 1) * 2 * rows, :] = block


def finish_kernel(chips, heads, core_ref, own_ref, other_ref, q_ref, do_ref, latn_ref, wk_ref, wv_ref, du_ref,
                  up_out, dl_out, dwq_out, dwk_out, dwv_out, dwo_out):
    lat, width = q_ref.shape
    feat = wk_ref.shape[0]
    half = own_ref.shape[0]
    rows = half // chips
    per = rows // heads
    core = core_ref[0]

    def place(at):
        c = jnp.where(at < half, core, 1 - core)
        chip = (at % half) // rows
        return (c * chips + chip) * per + at % per, (at % rows) // per

    both = jnp.concatenate([own_ref[...], other_ref[...]], axis=0)
    f = both[:, 0:feat]
    g = both[:, feat:2 * feat]
    ud = both[:, 2 * feat:]
    l, _ = place(iota((2 * half, lat), 0))
    spread = one_hot(l == iota((2 * half, lat), 1))
    _, h = place(iota((2 * half, width), 0))
    mine = h == iota((2 * half, width), 1) // HS
    zero = jnp.zeros((), f32)
    do = jnp.where(mine, nn(spread, do_ref[...]), zero).astype(bf16)
    q = jnp.where(mine, nn(spread, q_ref[...]), zero).astype(bf16)
    dwv_out[...] = tn(f, do)
    dwk_out[...] = tn(g, q)
    o = jnp.where(mine, nn(f, wv_ref[...]), zero).astype(bf16)
    dq = jnp.where(mine, nn(g, wk_ref[...]) * (HS ** -0.5), zero).astype(bf16)
    l, h = place(iota((lat, 2 * half), 1))
    hit = l == iota((lat, 2 * half), 0)
    gather = one_hot(hit)
    o = nn(gather, o).astype(bf16)
    dq = nn(gather, dq).astype(bf16)
    dwo_out[...] = tn(o, du_ref[...])
    dwq_out[...] = tn(latn_ref[...], dq)
    up_out[...] = nn(one_hot(hit & (h == 0)), ud).astype(bf16)
    dl_out[...] = nn(one_hot(hit & (h == 1)), ud)


def small(kernel, outs, smem, name):
    one = pl.BlockSpec(memory_space=pltpu.VMEM)
    params = pltpu.CompilerParams(vmem_limit_bytes=VMEM)
    shapes = [jax.ShapeDtypeStruct(s, t) for s, t in outs]

    def call(*args):
        specs = [pl.BlockSpec(memory_space=pltpu.SMEM)] * smem + [one] * (len(args) - smem)
        return pl.pallas_call(
            kernel, out_shape=shapes, in_specs=specs, out_specs=[one] * len(shapes), compiler_params=params, name=name
        )(*args)

    return call


def shards(tokens, coords, latents, anchors, gamma, w_query, w_key, w_value, w_out, d_update):
    lat, dl = latents.shape
    feat = tokens.shape[1]
    heads = gamma.shape[0]
    width = heads * HS
    chips = lax.axis_size("chip")
    groups = lax.axis_size("head")
    half = heads * lat // 2
    rows = half // chips
    wide = 2 * feat
    core = lax.axis_index("core").astype(jnp.int32).reshape(1)
    chip = lax.axis_index("chip").astype(jnp.int32).reshape(1)
    swap = [(0, 1), (1, 0)]

    send, keep, latn, q, do, r = token_pass(
        core, gamma, tokens, coords, latents, anchors, w_query, w_key, w_value, w_out, d_update
    )
    got = lax.ppermute(send, "core", swap)
    (pair,) = small(pair_kernel, [((half, wide + STAT), bf16)], 0, "pair_sum")(keep, got)
    shares = lax.all_to_all(pair.reshape(chips, rows, wide + STAT), "chip", 0, 0, tiled=True)
    fg, part = small(
        functools.partial(owner_kernel, lat, heads, chips), [((rows, wide), bf16), ((rows, dl), bf16)], 2, "owner_rows"
    )(core, chip, shares.reshape(half, wide + STAT), r, w_key, w_value, w_out, w_query)
    parts = [part]
    for k in range(1, groups):
        parts.append(lax.ppermute(part, "head", [(i, (i + k) % groups) for i in range(groups)]))
    (copies,) = small(
        functools.partial(spread_kernel, chips, heads, groups), [((half, wide + dl), bf16)], 2, "spread_rows"
    )(core, chip, *parts, fg, latents)
    own = lax.all_to_all(copies.reshape(chips, rows, wide + dl), "chip", 0, 0, tiled=True).reshape(half, wide + dl)
    other = lax.ppermute(own, "core", swap)
    outs = [((lat, dl), bf16), ((lat, dl), f32), ((dl, width), f32), ((feat, width), f32), ((feat, width), f32), ((width, dl), f32)]
    return tuple(
        small(functools.partial(finish_kernel, chips, heads), outs, 1, "finish")(
            core, own, other, q, do, latn, w_key, w_value, d_update
        )
    )


def solution(mesh):
    toks, head = mesh.devices.shape
    fine = Mesh(mesh.devices.reshape(toks // 2, 2, head), ("chip", "core", "head"))
    tok = ("chip", "core")
    return jax.shard_map(
        shards,
        mesh=fine,
        in_specs=(
            P(tok, None),
            P(None, tok),
            P(),
            P(),
            P("head"),
            P(None, "head"),
            P(None, "head"),
            P(None, "head"),
            P("head", None),
            P(),
        ),
        out_specs=(P(), P(), P(None, "head"), P(None, "head"), P(None, "head"), P("head", None)),
        check_vma=False,
    )
```

time: 94.7 us -> 82.7 us (0.87)
  blocking collectives: 40.5 us -> 18 us
  waiting for transfers between devices: 6.32 us -> 18.9 us
  Pallas kernels: 31.6 us -> 21 us
  starting transfers between devices: 12.4 us -> 21.9 us
    all_to_all x1 -> x0, blocking collectives: 22.3 us -> none  [shards(): lax.all_to_all(pair.reshape(chips, rows, wide + STAT), 'chip', 0, 0, tile...]
    all_to_all x0 -> x1, waiting for transfers between devices: none -> 12.8 us  [shards(): lax.all_to_all(pair.reshape(chips, rows, wide + STAT), 'chip', 0, 0, tile...]
    all_to_all x0 -> x1, starting transfers between devices: none -> 9.47 us  [shards(): lax.all_to_all(pair.reshape(chips, rows, wide + STAT), 'chip', 0, 0, tile...]
    pallas_call x4, Pallas kernels: 10.7 us -> 4.56 us  [call(): pl.pallas_call(kernel, out_shape=shapes, in_specs=specs, out_specs=[one]...]
    pallas_call x1, Pallas kernels: 21 us -> 16.4 us  [token_pass(): pl.pallas_call(functools.partial(token_kernel, lat, heads, tb, tc), grid=...]
    unnamed x12 -> x22, local copies, waits for them, and re-layouts: 2.12 us -> 1.95 us
  transfers between devices with their start and end apart: 5 -> 6, of which waited for: 4 -> 5; matrix products, arithmetic and copies ran while one was open for 0% -> 0% of each run, Pallas kernels for 0% -> 0%
where the time goes in v2:
time: 82.7 us; the launch traced here: 82.4 us
  starting transfers between devices  21.9 us (26%)
  Pallas kernels  21 us (25%)
  waiting for transfers between devices  18.9 us (23%)
  blocking collectives  18 us (22%)
  local copies, waits for them, and re-layouts  1.95 us (2%)
    all_to_all x1, blocking collectives, shards(): lax.all_to_all(copies.reshape(chips, rows, wide + dl), 'chip', 0, 0, tile...  18 us
    pallas_call x1, Pallas kernels, token_pass(): pl.pallas_call(functools.partial(token_kernel, lat, heads, tb, tc), grid=...  16.4 us
    all_to_all x1, waiting for transfers between devices, shards(): lax.all_to_all(pair.reshape(chips, rows, wide + STAT), 'chip', 0, 0, tile...  12.8 us
    all_to_all x1, starting transfers between devices, shards(): lax.all_to_all(pair.reshape(chips, rows, wide + STAT), 'chip', 0, 0, tile...  9.47 us
    ppermute x1, starting transfers between devices, shards(): other = lax.ppermute(own, 'core', swap)  5.56 us
    pallas_call x4, Pallas kernels, call(): pl.pallas_call(kernel, out_shape=shapes, in_specs=specs, out_specs=[one]...  4.56 us
    ppermute x3, starting transfers between devices, shards(): lax.ppermute(part, 'head', [(i, (i + k) % groups) for i in range(groups)])  3.64 us
    ppermute x1, starting transfers between devices, shards(): got = lax.ppermute(send, 'core', swap)  3.25 us
  transfers between devices with their start and end apart: 6, of which 5 were waited for; matrix products, arithmetic and copies ran while one was open for 0% of the time, Pallas kernels for 0%

profile of v2, /device:TPU:1, one launch (start us, length us, event | category | flops | bytes accessed | tf_op | source)
XLA Modules:
  0.0 82.4 jit_solution(12372247591521850458)
XLA Ops:
  0.6 0.0 copy-start.3
  0.6 0.0 copy-start.2
  0.7 0.0 copy-start.5
  0.7 0.0 copy-start.4
  0.7 0.0 copy-start
  0.7 0.0 copy-start.1
  0.7 16.4 %token_pass.1 = (bf16[256,640]{1,0:T(8,128)(2,1)}, bf16[256,640]{1,0:T(8,128)(2,1)}, bf16[256,512]{1,0:T(8,128)(2,1)}, bf16[256,128]{1,0:T(8,128)(2,1)}, bf16[25...) custom-call(s32[1]{0:T(128)} %bitcast.core_ref, f32[2]{0:T(128)} %gamma_ref.1, bf16[8192,256]{1,0:T(8,128)(2,1)} %tok_ref.1, ...), custom_call_target="tpu_custom_call" | custom-call | tf_op jit(solution)/shard_map/token_pass/pallas_call | solution.py:186
  17.1 3.2 %collective-permute-start = (bf16[256,640]{1,0:T(8,128)(2,1)}, bf16[256,640]{1,0:T(8,128)(2,1)S(1)}, u32[]{:S(2)}, u32[]{:S(2)}) collective-permute-start(bf16[256,640]{1,0:T(8,128)(2,1)} %get-tuple-element.15), channel_id=1, source_target_pairs={{0,4},{4,0},{1,5},{5,1},{2,6},{6,2},{3,7},{7,3},{8,12},{12,8},{9,1... | collective-permute-start | bytes 983048 | tf_op jit(solution)/shard_map/ppermute | solution.py:359
  20.4 1.5 %collective-permute-done.b_ref = bf16[256,640]{1,0:T(8,128)(2,1)S(1)} collective-permute-done((bf16[256,640]{1,0:T(8,128)(2,1)}, bf16[256,640]{1,0:T(8,128)(2,1)S(1)}, u32[]{:S(2)}, u32[]{:S(2)}) %collective-permute-start) | collective-permute-done | bytes 327712 | tf_op jit(solution)/shard_map/ppermute | solution.py:359
  21.8 1.0 %copy-done.6 = bf16[256,640]{1,0:T(8,128)(2,1)S(1)} copy-done((bf16[256,640]{1,0:T(8,128)(2,1)S(1)}, bf16[256,640]{1,0:T(8,128)(2,1)}, u32[]{:S(2)}) %copy-start.6) | copy-done | bytes 327704
  22.8 1.2 %pair_sum.1 = bf16[256,640]{1,0:T(8,128)(2,1)} custom-call(bf16[256,640]{1,0:T(8,128)(2,1)S(1)} %copy-done.6, bf16[256,640]{1,0:T(8,128)(2,1)S(1)} %collective-permute-done.b_ref), custom_call_target="tpu_custom_call" | custom-call | tf_op jit(solution)/shard_map/pair_sum/pallas_call | solution.py:335
  24.0 9.5 %all-to-all-start = ((bf16[32,8,640]{2,1,0:T(8,128)(2,1)}), bf16[32,8,640]{2,1,0:T(8,128)(2,1)S(1)}, u32[]{:S(2)}, u32[]{:S(2)}) async-start(bf16[32,8,640]{2,1,0:T(8,128)(2,1)} %bitcast.2), calls=%async_computation | async-start | bytes 655360 | tf_op jit(solution)/shard_map/all_to_all | solution.py:361
  33.4 12.8 %all-to-all-done = bf16[32,8,640]{2,1,0:T(8,128)(2,1)S(1)} async-done(((bf16[32,8,640]{2,1,0:T(8,128)(2,1)}), bf16[32,8,640]{2,1,0:T(8,128)(2,1)S(1)}, u32[]{:S(2)}, u32[]{:S(2)}) %all-to-all-start) | async-done | bytes 327712 | tf_op jit(solution)/shard_map/all_to_all | solution.py:361
  46.2 0.0 copy-done.3
  46.2 0.0 copy-done.2
  46.2 0.0 copy-start.7
  46.2 0.9 %copy-done.7 = bf16[512,256]{1,0:T(8,128)(2,1)S(1)} copy-done((bf16[512,256]{1,0:T(8,128)(2,1)S(1)}, bf16[512,256]{1,0:T(8,128)(2,1)}, u32[]{:S(2)}) %copy-start.7) | copy-done | bytes 262168
  47.2 0.6 owner_rows.1
  47.7 2.5 %collective-permute-start.3 = (bf16[8,512]{1,0:T(8,128)(2,1)S(1)}, bf16[8,512]{1,0:T(8,128)(2,1)S(1)}, u32[]{:S(2)}, u32[]{:S(2)}) collective-permute-start(bf16[8,512]{1,0:T(8,128)(2,1)S(1)} %get-tuple-element.17.refs_0_), channel_id=1, source_target_pairs={{0,3},{1,0},{2,1},{3,2},{4,7},{5,4},{6,5},{7,6},{8,11},{9,8},{10,9... | collective-permute-start | bytes 24584 | tf_op jit(solution)/shard_map/ppermute | solution.py:367
  50.2 0.5 collective-permute-start.2
  50.8 0.6 collective-permute-start.1
  51.4 0.0 collective-permute-done.3.refs_3_
  51.4 2.9 %collective-permute-done.2.refs_2_ = bf16[8,512]{1,0:T(8,128)(2,1)S(1)} collective-permute-done((bf16[8,512]{1,0:T(8,128)(2,1)S(1)}, bf16[8,512]{1,0:T(8,128)(2,1)S(1)}, u32[]{:S(2)}, u32[]{:S(2)}) %collective-permute-start.2) | collective-permute-done | bytes 8224 | tf_op jit(solution)/shard_map/ppermute | solution.py:367
  54.2 0.2 collective-permute-done.1.refs_1_
  54.5 0.0 copy-done
  54.5 0.4 spread_rows.1
  54.9 18.0 %all_to_all.10 = bf16[32,8,1024]{2,1,0:T(8,128)(2,1)S(1)} all-to-all(bf16[32,8,1024]{2,1,0:T(8,128)(2,1)S(1)} %bitcast.6), channel_id=1, replica_groups=mesh['chip'=32,'core'=2,'head'=4] {'chip'}, dimensions={0} | all-to-all | bytes 1048576 | tf_op jit(solution)/shard_map/all_to_all | solution.py:371
  72.9 5.6 %collective-permute-start.4 = (bf16[256,1024]{1,0:T(8,128)(2,1)S(1)}, bf16[256,1024]{1,0:T(8,128)(2,1)S(1)}, u32[]{:S(2)}, u32[]{:S(2)}) collective-permute-start(bf16[256,1024]{1,0:T(8,128)(2,1)S(1)} %bitcast.7), channel_id=1, source_target_pairs={{0,4},{4,0},{1,5},{5,1},{2,6},{6,2},{3,7},{7,3},{8,12},{12,8},{9,1... | collective-permute-start | bytes 1572872 | tf_op jit(solution)/shard_map/ppermute | solution.py:372
  78.4 1.5 %collective-permute-done.4.other_ref = bf16[256,1024]{1,0:T(8,128)(2,1)S(1)} collective-permute-done((bf16[256,1024]{1,0:T(8,128)(2,1)S(1)}, bf16[256,1024]{1,0:T(8,128)(2,1)S(1)}, u32[]{:S(2)}, u32[]{:S(2)}) %collective-permute-start.4) | collective-permute-done | bytes 524320 | tf_op jit(solution)/shard_map/ppermute | solution.py:372
  80.0 0.0 copy-done.8
  80.0 0.0 copy-done.10
  80.0 2.4 %finish.1 = (bf16[256,512]{1,0:T(8,128)(2,1)}, f32[256,512]{1,0:T(8,128)}, f32[512,128]{1,0:T(8,128)}, f32[256,128]{1,0:T(8,128)}, f32[256,128]{1,0:T(8,128)}, /*index=5*/f32[128,512]{1,0:T(8,128)}) custom-call(s32[1]{0:T(128)} %bitcast.core_ref, bf16[256,1024]{1,0:T(8,128)(2,1)S(1)} %bitcast.8, bf16[256,1024]{1,0:T(8,128)(2,1)S(1)} %collective-permute-done.4.other_ref, ...), custom_call_target="tpu_custom_call" | custom-call | tf_op jit(solution)/shard_map/finish/pallas_call | solution.py:335
  (8 shorter events, 0.0 us)
Async XLA Ops:
  0.6 45.6 %copy-start.3 = (bf16[256,128]{1,0:T(8,128)(2,1)S(1)}, bf16[256,128]{1,0:T(8,128)(2,1)}, u32[]{:S(2)}) copy-start(bf16[256,128]{1,0:T(8,128)(2,1)} %wv_ref.5) | copy-start | bytes 196612
  0.6 45.6 %copy-start.2 = (bf16[256,128]{1,0:T(8,128)(2,1)S(1)}, bf16[256,128]{1,0:T(8,128)(2,1)}, u32[]{:S(2)}) copy-start(bf16[256,128]{1,0:T(8,128)(2,1)} %wk_ref.5) | copy-start | bytes 196612
  0.7 45.5 %copy-start.5 = (bf16[128,512]{1,0:T(8,128)(2,1)S(1)}, bf16[128,512]{1,0:T(8,128)(2,1)}, u32[]{:S(2)}) copy-start(bf16[128,512]{1,0:T(8,128)(2,1)} %wo_ref.3) | copy-start | bytes 393220
  0.7 45.5 %copy-start.4 = (bf16[512,128]{1,0:T(8,128)(2,1)S(1)}, bf16[512,128]{1,0:T(8,128)(2,1)}, u32[]{:S(2)}) copy-start(bf16[512,128]{1,0:T(8,128)(2,1)} %wq_ref.3) | copy-start | bytes 393220
  0.7 53.8 %copy-start = (bf16[256,512]{1,0:T(8,128)(2,1)S(1)}, bf16[256,512]{1,0:T(8,128)(2,1)}, u32[]{:S(2)}) copy-start(bf16[256,512]{1,0:T(8,128)(2,1)} %refs_5_.1) | copy-start | bytes 786436
  0.7 79.3 %copy-start.1 = (bf16[256,512]{1,0:T(8,128)(2,1)S(1)}, bf16[256,512]{1,0:T(8,128)(2,1)}, u32[]{:S(2)}) copy-start(bf16[256,512]{1,0:T(8,128)(2,1)} %du_ref.3) | copy-start | bytes 786436
  17.1 4.7 %collective-permute-start = (bf16[256,640]{1,0:T(8,128)(2,1)}, bf16[256,640]{1,0:T(8,128)(2,1)S(1)}, u32[]{:S(2)}, u32[]{:S(2)}) collective-permute-start(bf16[256,640]{1,0:T(8,128)(2,1)} %get-tuple-element.15), channel_id=1, source_target_pairs={{0,4},{4,0},{1,5},{5,1},{2,6},{6,2},{3,7},{7,3},{8,12},{12,8},{9,1... | collective-permute-start | bytes 983048 | tf_op jit(solution)/shard_map/ppermute | solution.py:359
  21.8 1.0 %copy-start.6 = (bf16[256,640]{1,0:T(8,128)(2,1)S(1)}, bf16[256,640]{1,0:T(8,128)(2,1)}, u32[]{:S(2)}) copy-start(bf16[256,640]{1,0:T(8,128)(2,1)} %get-tuple-element.14.a_ref) | copy-start | bytes 983044
  22.8 57.2 %copy-start.8 = (bf16[256,512]{1,0:T(8,128)(2,1)S(1)}, bf16[256,512]{1,0:T(8,128)(2,1)}, u32[]{:S(2)}) copy-start(bf16[256,512]{1,0:T(8,128)(2,1)} %get-tuple-element.21.latn_ref) | copy-start | bytes 786436
  22.8 57.2 %copy-start.9 = (bf16[256,128]{1,0:T(8,128)(2,1)S(1)}, bf16[256,128]{1,0:T(8,128)(2,1)}, u32[]{:S(2)}) copy-start(bf16[256,128]{1,0:T(8,128)(2,1)} %get-tuple-element.19.q_ref) | copy-start | bytes 196612
  22.8 57.2 %copy-start.10 = (bf16[256,128]{1,0:T(8,128)(2,1)S(1)}, bf16[256,128]{1,0:T(8,128)(2,1)}, u32[]{:S(2)}) copy-start(bf16[256,128]{1,0:T(8,128)(2,1)} %get-tuple-element.20.do_ref) | copy-start | bytes 196612
  24.0 22.2 %all-to-all-start = ((bf16[32,8,640]{2,1,0:T(8,128)(2,1)}), bf16[32,8,640]{2,1,0:T(8,128)(2,1)S(1)}, u32[]{:S(2)}, u32[]{:S(2)}) async-start(bf16[32,8,640]{2,1,0:T(8,128)(2,1)} %bitcast.2), calls=%async_computation | async-start | bytes 655360 | tf_op jit(solution)/shard_map/all_to_all | solution.py:361
  46.2 1.0 %copy-start.7 = (bf16[512,256]{1,0:T(8,128)(2,1)S(1)}, bf16[512,256]{1,0:T(8,128)(2,1)}, u32[]{:S(2)}) copy-start(bf16[512,256]{1,0:T(8,128)(2,1)} %get-tuple-element.16.r_ref) | copy-start | bytes 786436
  47.7 3.6 %collective-permute-start.3 = (bf16[8,512]{1,0:T(8,128)(2,1)S(1)}, bf16[8,512]{1,0:T(8,128)(2,1)S(1)}, u32[]{:S(2)}, u32[]{:S(2)}) collective-permute-start(bf16[8,512]{1,0:T(8,128)(2,1)S(1)} %get-tuple-element.17.refs_0_), channel_id=1, source_target_pairs={{0,3},{1,0},{2,1},{3,2},{4,7},{5,4},{6,5},{7,6},{8,11},{9,8},{10,9... | collective-permute-start | bytes 24584 | tf_op jit(solution)/shard_map/ppermute | solution.py:367
  50.2 4.0 %collective-permute-start.2 = (bf16[8,512]{1,0:T(8,128)(2,1)S(1)}, bf16[8,512]{1,0:T(8,128)(2,1)S(1)}, u32[]{:S(2)}, u32[]{:S(2)}) collective-permute-start(bf16[8,512]{1,0:T(8,128)(2,1)S(1)} %get-tuple-element.17.refs_0_), channel_id=1, source_target_pairs={{0,2},{1,3},{2,0},{3,1},{4,6},{5,7},{6,4},{7,5},{8,10},{9,11},{10,... | collective-permute-start | bytes 24584 | tf_op jit(solution)/shard_map/ppermute | solution.py:367
  50.8 3.7 %collective-permute-start.1 = (bf16[8,512]{1,0:T(8,128)(2,1)S(1)}, bf16[8,512]{1,0:T(8,128)(2,1)S(1)}, u32[]{:S(2)}, u32[]{:S(2)}) collective-permute-start(bf16[8,512]{1,0:T(8,128)(2,1)S(1)} %get-tuple-element.17.refs_0_), channel_id=1, source_target_pairs={{0,1},{1,2},{2,3},{3,0},{4,5},{5,6},{6,7},{7,4},{8,9},{9,10},{10,1... | collective-permute-start | bytes 24584 | tf_op jit(solution)/shard_map/ppermute | solution.py:367
  72.9 7.1 %collective-permute-start.4 = (bf16[256,1024]{1,0:T(8,128)(2,1)S(1)}, bf16[256,1024]{1,0:T(8,128)(2,1)S(1)}, u32[]{:S(2)}, u32[]{:S(2)}) collective-permute-start(bf16[256,1024]{1,0:T(8,128)(2,1)S(1)} %bitcast.7), channel_id=1, source_target_pairs={{0,4},{4,0},{1,5},{5,1},{2,6},{6,2},{3,7},{7,3},{8,12},{12,8},{9,1... | collective-permute-start | bytes 1572872 | tf_op jit(solution)/shard_map/ppermute | solution.py:372

commit v3 on v2

--- a/solution.py
+++ b/solution.py
@@ -57,7 +57,7 @@
 
 
 def token_kernel(lat, heads, tb, tc, core_ref, gamma_ref, tok_ref, pts_ref, lat_ref, anc_ref, wq_ref, wk_ref, wv_ref,
-                 wo_ref, du_ref, send_ref, keep_ref, latn_out, q_out, do_out, r_out,
+                 wo_ref, du_ref, send_ref, keep_ref, latn_out, q_out, do_out,
                  anc_s, p_s, r_s, shift_s, x_s, acc_s, z_s):
     step = pl.program_id(0)
     steps = pl.num_programs(0)
@@ -87,7 +87,6 @@
             r = nt(jnp.where(mine, do, jnp.zeros((), bf16)), wv_ref[...]).astype(bf16)
             p_s[at, :] = p
             r_s[at, :] = r
-            r_out[at, :] = r
             size = p.astype(f32)
             size = jnp.sqrt(jnp.sum(size * size, axis=1, keepdims=True)) * (feat ** 0.5)
             shift_s[at, :] = jnp.broadcast_to(two_parts(size - gamma_ref[h] * box), (lat, 128))
@@ -180,7 +179,7 @@
         return pl.BlockSpec(a.shape, lambda i: (0,) * len(a.shape))
 
     smem = pl.BlockSpec(memory_space=pltpu.SMEM)
-    shapes = [(rows // 2, cols)] * 2 + [(lat, dl), (lat, width), (lat, width), (rows, feat)]
+    shapes = [(rows // 2, cols)] * 2 + [(lat, dl), (lat, width), (lat, width)]
     outs = [jax.ShapeDtypeStruct(s, bf16) for s in shapes]
     held = (coords, latents, anchors, wq, wk, wv, wo, du)
     return pl.pallas_call(
@@ -228,7 +227,7 @@
     out_ref[:, wide:] = write_stat(za * wa + zb * wb, shift)
 
 
-def owner_kernel(lat, heads, chips, core_ref, chip_ref, all_ref, r_ref, wk_ref, wv_ref, wo_ref, wq_ref, fg_out, part_out):
+def owner_kernel(lat, heads, chips, core_ref, chip_ref, all_ref, du_ref, wk_ref, wv_ref, wo_ref, wq_ref, fg_out, part_out):
     rows = all_ref.shape[0] // chips
     per = rows // heads
     feat = wk_ref.shape[0]
@@ -244,15 +243,16 @@
     sums = jnp.sum(all_ref[:, 0:wide].astype(f32).reshape(chips, rows, wide) * w, axis=0)
     inv = 1.0 / total
     f = sums[:, 0:feat] * inv
-    at = iota((rows, heads * lat), 0)
-    src = (at // per) * lat + group * per + at % per
-    r = nn(one_hot(iota((rows, heads * lat), 1) == src), r_ref[...])
+    at = iota((rows, lat), 0)
+    du = nn(one_hot(iota((rows, lat), 1) == group * per + at % per), du_ref[...]).astype(bf16)
+    mine = iota((rows, width), 1) // HS == iota((rows, width), 0) // per
+    do = jnp.where(mine, nt(du, wo_ref[...]), 0.0).astype(bf16)
+    r = nt(do, wv_ref[...]).astype(bf16).astype(f32)
     delta = jnp.sum(f * r, axis=1, keepdims=True)
     g = sums[:, feat:wide] * inv - delta * f
     fb = f.astype(bf16)
     gb = g.astype(bf16)
     fg_out[...] = jnp.concatenate([fb, gb], axis=1)
-    mine = iota((rows, width), 1) // HS == iota((rows, width), 0) // per
     o = jnp.where(mine, nn(fb, wv_ref[...]), 0.0).astype(bf16)
     dq = jnp.where(mine, nn(gb, wk_ref[...]) * (HS ** -0.5), 0.0).astype(bf16)
     up = nn(o, wo_ref[...])
@@ -285,44 +285,55 @@
         out_ref[s * 2 * rows:(s + 1) * 2 * rows, :] = block
 
 
-def finish_kernel(chips, heads, core_ref, own_ref, other_ref, q_ref, do_ref, latn_ref, wk_ref, wv_ref, du_ref,
-                  up_out, dl_out, dwq_out, dwk_out, dwv_out, dwo_out):
+def half_terms(chips, heads, core, rows_ref, q_ref, do_ref, wk_ref, wv_ref):
     lat, width = q_ref.shape
     feat = wk_ref.shape[0]
-    half = own_ref.shape[0]
+    half = rows_ref.shape[0]
     rows = half // chips
     per = rows // heads
-    core = core_ref[0]
-
-    def place(at):
-        c = jnp.where(at < half, core, 1 - core)
-        chip = (at % half) // rows
-        return (c * chips + chip) * per + at % per, (at % rows) // per
-
-    both = jnp.concatenate([own_ref[...], other_ref[...]], axis=0)
-    f = both[:, 0:feat]
-    g = both[:, feat:2 * feat]
-    ud = both[:, 2 * feat:]
-    l, _ = place(iota((2 * half, lat), 0))
-    spread = one_hot(l == iota((2 * half, lat), 1))
-    _, h = place(iota((2 * half, width), 0))
-    mine = h == iota((2 * half, width), 1) // HS
+
+    def latent(at):
+        return (core * chips + at // rows) * per + at % per
+
+    f = rows_ref[:, 0:feat]
+    g = rows_ref[:, feat:2 * feat]
+    ud = rows_ref[:, 2 * feat:]
+    spread = one_hot(latent(iota((half, lat), 0)) == iota((half, lat), 1))
+    mine = iota((half, width), 0) % rows // per == iota((half, width), 1) // HS
     zero = jnp.zeros((), f32)
     do = jnp.where(mine, nn(spread, do_ref[...]), zero).astype(bf16)
     q = jnp.where(mine, nn(spread, q_ref[...]), zero).astype(bf16)
-    dwv_out[...] = tn(f, do)
-    dwk_out[...] = tn(g, q)
     o = jnp.where(mine, nn(f, wv_ref[...]), zero).astype(bf16)
     dq = jnp.where(mine, nn(g, wk_ref[...]) * (HS ** -0.5), zero).astype(bf16)
-    l, h = place(iota((lat, 2 * half), 1))
-    hit = l == iota((lat, 2 * half), 0)
+    at = iota((lat, half), 1)
+    hit = latent(at) == iota((lat, half), 0)
     gather = one_hot(hit)
-    o = nn(gather, o).astype(bf16)
-    dq = nn(gather, dq).astype(bf16)
-    dwo_out[...] = tn(o, du_ref[...])
-    dwq_out[...] = tn(latn_ref[...], dq)
-    up_out[...] = nn(one_hot(hit & (h == 0)), ud).astype(bf16)
-    dl_out[...] = nn(one_hot(hit & (h == 1)), ud)
+    first = at % rows // per == 0
+    return (
+        tn(f, do),
+        tn(g, q),
+        nn(gather, o).astype(bf16),
+        nn(gather, dq).astype(bf16),
+        nn(one_hot(hit & first), ud).astype(bf16),
+        nn(one_hot(hit & (at % rows // per == 1)), ud),
+    )
+
+
+def finish_own_kernel(chips, heads, core_ref, own_ref, q_ref, do_ref, wk_ref, wv_ref, *outs):
+    for out, term in zip(outs, half_terms(chips, heads, core_ref[0], own_ref, q_ref, do_ref, wk_ref, wv_ref)):
+        out[...] = term
+
+
+def finish_kernel(chips, heads, core_ref, other_ref, q_ref, do_ref, wk_ref, wv_ref, latn_ref, du_ref,
+                  dwv_ref, dwk_ref, o_ref, dq_ref, up_ref, dl_ref,
+                  up_out, dl_out, dwq_out, dwk_out, dwv_out, dwo_out):
+    dwv, dwk, o, dq, up, dl = half_terms(chips, heads, 1 - core_ref[0], other_ref, q_ref, do_ref, wk_ref, wv_ref)
+    dwv_out[...] = dwv_ref[...] + dwv
+    dwk_out[...] = dwk_ref[...] + dwk
+    up_out[...] = up_ref[...] + up
+    dl_out[...] = dl_ref[...] + dl
+    dwo_out[...] = tn(o_ref[...] + o, du_ref[...])
+    dwq_out[...] = tn(latn_ref[...], dq_ref[...] + dq)
 
 
 def small(kernel, outs, smem, name):
@@ -333,7 +344,8 @@
     def call(*args):
         specs = [pl.BlockSpec(memory_space=pltpu.SMEM)] * smem + [one] * (len(args) - smem)
         return pl.pallas_call(
-            kernel, out_shape=shapes, in_specs=specs, out_specs=[one] * len(shapes), compiler_params=params, name=name
+            kernel, out_shape=shapes, in_specs=specs, out_specs=[one] * len(shapes), compiler_params=params, name=name,
+            cost_estimate=pl.CostEstimate(flops=4 * 10 ** 8, bytes_accessed=10 ** 6, transcendentals=0),
         )(*args)
 
     return call
@@ -353,15 +365,15 @@
     chip = lax.axis_index("chip").astype(jnp.int32).reshape(1)
     swap = [(0, 1), (1, 0)]
 
-    send, keep, latn, q, do, r = token_pass(
+    send, keep, latn, q, do = token_pass(
         core, gamma, tokens, coords, latents, anchors, w_query, w_key, w_value, w_out, d_update
     )
     got = lax.ppermute(send, "core", swap)
-    (pair,) = small(pair_kernel, [((half, wide + STAT), bf16)], 0, "pair_sum")(keep, got)
+    (pair,) = small(pair_kernel, [((half, wide + STAT), bf16)], 0, "pair_sum")(keep.astype(f32), got)
     shares = lax.all_to_all(pair.reshape(chips, rows, wide + STAT), "chip", 0, 0, tiled=True)
     fg, part = small(
         functools.partial(owner_kernel, lat, heads, chips), [((rows, wide), bf16), ((rows, dl), bf16)], 2, "owner_rows"
-    )(core, chip, shares.reshape(half, wide + STAT), r, w_key, w_value, w_out, w_query)
+    )(core, chip, shares.reshape(half, wide + STAT), d_update, w_key, w_value, w_out, w_query)
     parts = [part]
     for k in range(1, groups):
         parts.append(lax.ppermute(part, "head", [(i, (i + k) % groups) for i in range(groups)]))
@@ -370,10 +382,14 @@
     )(core, chip, *parts, fg, latents)
     own = lax.all_to_all(copies.reshape(chips, rows, wide + dl), "chip", 0, 0, tiled=True).reshape(half, wide + dl)
     other = lax.ppermute(own, "core", swap)
+    terms = [((feat, width), f32)] * 2 + [((lat, width), bf16)] * 2 + [((lat, dl), bf16), ((lat, dl), f32)]
+    mine = small(functools.partial(finish_own_kernel, chips, heads), terms, 1, "finish_own")(
+        core, own, q, do, w_key, w_value
+    )
     outs = [((lat, dl), bf16), ((lat, dl), f32), ((dl, width), f32), ((feat, width), f32), ((feat, width), f32), ((width, dl), f32)]
     return tuple(
         small(functools.partial(finish_kernel, chips, heads), outs, 1, "finish")(
-            core, own, other, q, do, latn, w_key, w_value, d_update
+            core, other, q, do, w_key, w_value, latn, d_update, *mine
         )
     )
 

time: 82.7 us -> 80.3 us (0.971)
  local copies, waits for them, and re-layouts: 1.95 us -> 0.04 us
  waiting for transfers between devices: 18.9 us -> 17.1 us
  other arithmetic: 0 us -> 1.06 us
    unnamed x22 -> x18, local copies, waits for them, and re-layouts: 1.95 us -> 0.04 us
    ppermute x1, waiting for transfers between devices: 1.47 us -> 0.4 us  [shards(): got = lax.ppermute(send, 'core', swap)]
    convert_element_type x0 -> x1, other arithmetic: none -> 1.06 us  [shards(): keep.astype(f32)]
    pallas_call x4 -> x5, Pallas kernels: 4.56 us -> 4.68 us  [call(): pl.pallas_call(kernel, out_shape=shapes, in_specs=specs, out_specs=[one]...]
  transfers between devices with their start and end apart: 6 -> 6, of which waited for: 5 -> 5; matrix products, arithmetic and copies ran while one was open for 0% -> 1% of each run, Pallas kernels for 0% -> 1%
where the time goes in v3:
time: 80.3 us; the launch traced here: 80 us
  starting transfers between devices  22 us (27%)
  Pallas kernels  21 us (26%)
  blocking collectives  18 us (22%)
  waiting for transfers between devices  17.1 us (21%)
  other arithmetic  1.06 us (1%)
    all_to_all x1, blocking collectives, shards(): lax.all_to_all(copies.reshape(chips, rows, wide + dl), 'chip', 0, 0, tile...  18 us
    pallas_call x1, Pallas kernels, token_pass(): pl.pallas_call(functools.partial(token_kernel, lat, heads, tb, tc), grid=...  16.4 us
    all_to_all x1, waiting for transfers between devices, shards(): lax.all_to_all(pair.reshape(chips, rows, wide + STAT), 'chip', 0, 0, tile...  12.8 us
    all_to_all x1, starting transfers between devices, shards(): lax.all_to_all(pair.reshape(chips, rows, wide + STAT), 'chip', 0, 0, tile...  9.47 us
    ppermute x1, starting transfers between devices, shards(): other = lax.ppermute(own, 'core', swap)  5.56 us
    pallas_call x5, Pallas kernels, call(): pl.pallas_call(kernel, out_shape=shapes, in_specs=specs, out_specs=[one]...  4.68 us
    ppermute x3, starting transfers between devices, shards(): lax.ppermute(part, 'head', [(i, (i + k) % groups) for i in range(groups)])  3.64 us
    ppermute x1, starting transfers between devices, shards(): got = lax.ppermute(send, 'core', swap)  3.33 us
  transfers between devices with their start and end apart: 6, of which 5 were waited for; matrix products, arithmetic and copies ran while one was open for 1% of the time, Pallas kernels for 1%

profile of v3, /device:TPU:1, one launch (start us, length us, event | category | flops | bytes accessed | tf_op | source)
XLA Modules:
  0.0 80.0 jit_solution(16040960039360237118)
XLA Ops:
  0.6 0.0 copy-start
  0.7 0.0 copy-start.1
  0.7 0.0 copy-start.2
  0.7 0.0 copy-start.5
  0.7 0.0 copy-start.6
  0.7 0.0 copy-start.3
  0.7 16.4 %token_pass.1 = (bf16[256,640]{1,0:T(8,128)(2,1)}, bf16[256,640]{1,0:T(8,128)(2,1)}, bf16[256,512]{1,0:T(8,128)(2,1)}, bf16[256,128]{1,0:T(8,128)(2,1)}, bf16[256,128]{1,0:T(8,128)(2,1)}) custom-call(s32[1]{0:T(128)} %bitcast.core_ref, f32[2]{0:T(128)} %gamma_ref.1, bf16[8192,256]{1,0:T(8,128)(2,1)} %tok_ref.1, f32[3,8192]{1,0:T(4,128)} %pts_ref.1, ...), custom_call_target="tpu_custom_call" | custom-call | tf_op jit(solution)/shard_map/token_pass/pallas_call | solution.py:185
  17.1 3.3 %collective-permute-start = (bf16[256,640]{1,0:T(8,128)(2,1)}, bf16[256,640]{1,0:T(8,128)(2,1)S(1)}, u32[]{:S(2)}, u32[]{:S(2)}) collective-permute-start(bf16[256,640]{1,0:T(8,128)(2,1)} %get-tuple-element.20), channel_id=1, source_target_pairs={{0,4},{4,0},{1,5},{5,1},{2,6},{6,2},{3,7},{7,3},{8,12},{12,8},{9,1... | collective-permute-start | bytes 983048 | tf_op jit(solution)/shard_map/ppermute | solution.py:371
  20.4 1.1 %convert_element_type.3.a_ref = f32[256,640]{1,0:T(8,128)S(1)} convert(bf16[256,640]{1,0:T(8,128)(2,1)} %get-tuple-element.19) | non-fusion elementwise | flops 163840 | bytes 983040 | tf_op jit(solution)/shard_map/convert_element_type | solution.py:372
  21.5 0.4 collective-permute-done.b_ref
  21.9 1.2 %pair_sum.1 = bf16[256,640]{1,0:T(8,128)(2,1)} custom-call(f32[256,640]{1,0:T(8,128)S(1)} %convert_element_type.3.a_ref, bf16[256,640]{1,0:T(8,128)(2,1)S(1)} %collective-permute-done.b_ref), custom_call_target="tpu_custom_call" | custom-call | flops 400000000 | bytes 1000000 | tf_op jit(solution)/shard_map/pair_sum/pallas_call | solution.py:346
  23.0 9.5 %all-to-all-start = ((bf16[32,8,640]{2,1,0:T(8,128)(2,1)}), bf16[32,8,640]{2,1,0:T(8,128)(2,1)S(1)}, u32[]{:S(2)}, u32[]{:S(2)}) async-start(bf16[32,8,640]{2,1,0:T(8,128)(2,1)} %bitcast.2), calls=%async_computation | async-start | bytes 655360 | tf_op jit(solution)/shard_map/all_to_all | solution.py:373
  32.5 12.8 %all-to-all-done = bf16[32,8,640]{2,1,0:T(8,128)(2,1)S(1)} async-done(((bf16[32,8,640]{2,1,0:T(8,128)(2,1)}), bf16[32,8,640]{2,1,0:T(8,128)(2,1)S(1)}, u32[]{:S(2)}, u32[]{:S(2)}) %all-to-all-start) | async-done | bytes 327712 | tf_op jit(solution)/shard_map/all_to_all | solution.py:373
  45.3 0.0 copy-done
  45.3 0.0 copy-done.1
  45.3 0.0 copy-done.2
  45.3 0.0 copy-done.5
  45.3 0.0 copy-done.6
  45.3 0.7 owner_rows.1
  46.0 2.5 %collective-permute-start.3 = (bf16[8,512]{1,0:T(8,128)(2,1)S(1)}, bf16[8,512]{1,0:T(8,128)(2,1)S(1)}, u32[]{:S(2)}, u32[]{:S(2)}) collective-permute-start(bf16[8,512]{1,0:T(8,128)(2,1)S(1)} %get-tuple-element.21.refs_0_), channel_id=1, source_target_pairs={{0,3},{1,0},{2,1},{3,2},{4,7},{5,4},{6,5},{7,6},{8,11},{9,8},{10,9... | collective-permute-start | bytes 24584 | tf_op jit(solution)/shard_map/ppermute | solution.py:379
  48.5 0.5 collective-permute-start.2
  49.0 0.6 collective-permute-start.1
  49.6 0.0 collective-permute-done.3.refs_3_
  49.6 2.9 %collective-permute-done.2.refs_2_ = bf16[8,512]{1,0:T(8,128)(2,1)S(1)} collective-permute-done((bf16[8,512]{1,0:T(8,128)(2,1)S(1)}, bf16[8,512]{1,0:T(8,128)(2,1)S(1)}, u32[]{:S(2)}, u32[]{:S(2)}) %collective-permute-start.2) | collective-permute-done | bytes 8224 | tf_op jit(solution)/shard_map/ppermute | solution.py:379
  52.5 0.2 collective-permute-done.1.refs_1_
  52.7 0.4 spread_rows.1
  53.2 18.0 %all_to_all.10 = bf16[32,8,1024]{2,1,0:T(8,128)(2,1)S(1)} all-to-all(bf16[32,8,1024]{2,1,0:T(8,128)(2,1)S(1)} %bitcast.8), channel_id=1, replica_groups=mesh['chip'=32,'core'=2,'head'=4] {'chip'}, dimensions={0} | all-to-all | bytes 1048576 | tf_op jit(solution)/shard_map/all_to_all | solution.py:383
  71.2 5.6 %collective-permute-start.4 = (bf16[256,1024]{1,0:T(8,128)(2,1)S(1)}, bf16[256,1024]{1,0:T(8,128)(2,1)S(1)}, u32[]{:S(2)}, u32[]{:S(2)}) collective-permute-start(bf16[256,1024]{1,0:T(8,128)(2,1)S(1)} %bitcast.6), channel_id=1, source_target_pairs={{0,4},{4,0},{1,5},{5,1},{2,6},{6,2},{3,7},{7,3},{8,12},{12,8},{9,1... | collective-permute-start | bytes 1572872 | tf_op jit(solution)/shard_map/ppermute | solution.py:384
  76.7 0.0 copy-done.8
  76.7 0.6 finish_own.1
  77.4 0.9 %collective-permute-done.4.other_ref = bf16[256,1024]{1,0:T(8,128)(2,1)S(1)} collective-permute-done((bf16[256,1024]{1,0:T(8,128)(2,1)S(1)}, bf16[256,1024]{1,0:T(8,128)(2,1)S(1)}, u32[]{:S(2)}, u32[]{:S(2)}) %collective-permute-start.4) | collective-permute-done | bytes 524320 | tf_op jit(solution)/shard_map/ppermute | solution.py:384
  78.3 1.8 %finish.1 = (bf16[256,512]{1,0:T(8,128)(2,1)}, f32[256,512]{1,0:T(8,128)}, f32[512,128]{1,0:T(8,128)}, f32[256,128]{1,0:T(8,128)}, f32[256,128]{1,0:T(8,128)}, /*index=5*/f32[128,512]{1,0:T(8,128)}) custom-call(s32[1]{0:T(128)} %bitcast.core_ref, bf16[256,1024]{1,0:T(8,128)(2,1)S(1)} %collective-permute-done.4.other_ref, bf16[256,128]{1,0:T(8,128)(2,1)S(1)} %copy-done.7, ...), custom_call_target="tpu_custom_call" | custom-call | flops 400000000 | bytes 1000000 | tf_op jit(solution)/shard_map/finish/pallas_call | solution.py:346
  (6 shorter events, 0.0 us)
Async XLA Ops:
  0.6 44.6 %copy-start = (bf16[256,512]{1,0:T(8,128)(2,1)S(1)}, bf16[256,512]{1,0:T(8,128)(2,1)}, u32[]{:S(2)}) copy-start(bf16[256,512]{1,0:T(8,128)(2,1)} %du_ref.5) | copy-start | bytes 786436
  0.7 44.6 %copy-start.1 = (bf16[256,128]{1,0:T(8,128)(2,1)S(1)}, bf16[256,128]{1,0:T(8,128)(2,1)}, u32[]{:S(2)}) copy-start(bf16[256,128]{1,0:T(8,128)(2,1)} %wk_ref.7) | copy-start | bytes 196612
  0.7 44.6 %copy-start.2 = (bf16[256,128]{1,0:T(8,128)(2,1)S(1)}, bf16[256,128]{1,0:T(8,128)(2,1)}, u32[]{:S(2)}) copy-start(bf16[256,128]{1,0:T(8,128)(2,1)} %wv_ref.7) | copy-start | bytes 196612
  0.7 44.6 %copy-start.5 = (bf16[512,128]{1,0:T(8,128)(2,1)S(1)}, bf16[512,128]{1,0:T(8,128)(2,1)}, u32[]{:S(2)}) copy-start(bf16[512,128]{1,0:T(8,128)(2,1)} %wq_ref.3) | copy-start | bytes 393220
  0.7 44.6 %copy-start.6 = (bf16[128,512]{1,0:T(8,128)(2,1)S(1)}, bf16[128,512]{1,0:T(8,128)(2,1)}, u32[]{:S(2)}) copy-start(bf16[128,512]{1,0:T(8,128)(2,1)} %wo_ref.3) | copy-start | bytes 393220
  0.7 52.1 %copy-start.3 = (bf16[256,512]{1,0:T(8,128)(2,1)S(1)}, bf16[256,512]{1,0:T(8,128)(2,1)}, u32[]{:S(2)}) copy-start(bf16[256,512]{1,0:T(8,128)(2,1)} %refs_5_.1) | copy-start | bytes 786436
  17.1 59.7 %copy-start.7 = (bf16[256,128]{1,0:T(8,128)(2,1)S(1)}, bf16[256,128]{1,0:T(8,128)(2,1)}, u32[]{:S(2)}) copy-start(bf16[256,128]{1,0:T(8,128)(2,1)} %get-tuple-element.23.q_ref) | copy-start | bytes 196612
  17.1 59.7 %copy-start.8 = (bf16[256,128]{1,0:T(8,128)(2,1)S(1)}, bf16[256,128]{1,0:T(8,128)(2,1)}, u32[]{:S(2)}) copy-start(bf16[256,128]{1,0:T(8,128)(2,1)} %get-tuple-element.24.do_ref) | copy-start | bytes 196612
  17.1 4.8 %collective-permute-start = (bf16[256,640]{1,0:T(8,128)(2,1)}, bf16[256,640]{1,0:T(8,128)(2,1)S(1)}, u32[]{:S(2)}, u32[]{:S(2)}) collective-permute-start(bf16[256,640]{1,0:T(8,128)(2,1)} %get-tuple-element.20), channel_id=1, source_target_pairs={{0,4},{4,0},{1,5},{5,1},{2,6},{6,2},{3,7},{7,3},{8,12},{12,8},{9,1... | collective-permute-start | bytes 983048 | tf_op jit(solution)/shard_map/ppermute | solution.py:371
  20.4 57.9 %copy-start.4 = (bf16[256,512]{1,0:T(8,128)(2,1)S(1)}, bf16[256,512]{1,0:T(8,128)(2,1)}, u32[]{:S(2)}) copy-start(bf16[256,512]{1,0:T(8,128)(2,1)} %get-tuple-element.25.latn_ref) | copy-start | bytes 786436
  23.0 22.2 %all-to-all-start = ((bf16[32,8,640]{2,1,0:T(8,128)(2,1)}), bf16[32,8,640]{2,1,0:T(8,128)(2,1)S(1)}, u32[]{:S(2)}, u32[]{:S(2)}) async-start(bf16[32,8,640]{2,1,0:T(8,128)(2,1)} %bitcast.2), calls=%async_computation | async-start | bytes 655360 | tf_op jit(solution)/shard_map/all_to_all | solution.py:373
  46.0 3.6 %collective-permute-start.3 = (bf16[8,512]{1,0:T(8,128)(2,1)S(1)}, bf16[8,512]{1,0:T(8,128)(2,1)S(1)}, u32[]{:S(2)}, u32[]{:S(2)}) collective-permute-start(bf16[8,512]{1,0:T(8,128)(2,1)S(1)} %get-tuple-element.21.refs_0_), channel_id=1, source_target_pairs={{0,3},{1,0},{2,1},{3,2},{4,7},{5,4},{6,5},{7,6},{8,11},{9,8},{10,9... | collective-permute-start | bytes 24584 | tf_op jit(solution)/shard_map/ppermute | solution.py:379
  48.5 4.0 %collective-permute-start.2 = (bf16[8,512]{1,0:T(8,128)(2,1)S(1)}, bf16[8,512]{1,0:T(8,128)(2,1)S(1)}, u32[]{:S(2)}, u32[]{:S(2)}) collective-permute-start(bf16[8,512]{1,0:T(8,128)(2,1)S(1)} %get-tuple-element.21.refs_0_), channel_id=1, source_target_pairs={{0,2},{1,3},{2,0},{3,1},{4,6},{5,7},{6,4},{7,5},{8,10},{9,11},{10,... | collective-permute-start | bytes 24584 | tf_op jit(solution)/shard_map/ppermute | solution.py:379
  49.0 3.7 %collective-permute-start.1 = (bf16[8,512]{1,0:T(8,128)(2,1)S(1)}, bf16[8,512]{1,0:T(8,128)(2,1)S(1)}, u32[]{:S(2)}, u32[]{:S(2)}) collective-permute-start(bf16[8,512]{1,0:T(8,128)(2,1)S(1)} %get-tuple-element.21.refs_0_), channel_id=1, source_target_pairs={{0,1},{1,2},{2,3},{3,0},{4,5},{5,6},{6,7},{7,4},{8,9},{9,10},{10,1... | collective-permute-start | bytes 24584 | tf_op jit(solution)/shard_map/ppermute | solution.py:379
  71.2 7.1 %collective-permute-start.4 = (bf16[256,1024]{1,0:T(8,128)(2,1)S(1)}, bf16[256,1024]{1,0:T(8,128)(2,1)S(1)}, u32[]{:S(2)}, u32[]{:S(2)}) collective-permute-start(bf16[256,1024]{1,0:T(8,128)(2,1)S(1)} %bitcast.6), channel_id=1, source_target_pairs={{0,4},{4,0},{1,5},{5,1},{2,6},{6,2},{3,7},{7,3},{8,12},{12,8},{9,1... | collective-permute-start | bytes 1572872 | tf_op jit(solution)/shard_map/ppermute | solution.py:384

commit v4 on v3

--- a/solution.py
+++ b/solution.py
@@ -88,7 +88,7 @@
             p_s[at, :] = p
             r_s[at, :] = r
             size = p.astype(f32)
-            size = jnp.sqrt(jnp.sum(size * size, axis=1, keepdims=True)) * (feat ** 0.5)
+            size = jnp.sqrt(jnp.sum(size * size, axis=1, keepdims=True)) * (feat ** 0.5 * (1 + 2 ** -8))
             shift_s[at, :] = jnp.broadcast_to(two_parts(size - gamma_ref[h] * box), (lat, 128))
         acc_s[...] = jnp.zeros_like(acc_s)
         z_s[...] = jnp.zeros_like(z_s)

time: 80.3 us -> 80.3 us (level)
  no operation moved by 1% of the time
where the time goes in v4:
time: 80.3 us; the launch traced here: 80 us
  starting transfers between devices  22 us (27%)
  Pallas kernels  21 us (26%)
  blocking collectives  18 us (22%)
  waiting for transfers between devices  17.1 us (21%)
  other arithmetic  1.06 us (1%)
    all_to_all x1, blocking collectives, shards(): lax.all_to_all(copies.reshape(chips, rows, wide + dl), 'chip', 0, 0, tile...  18 us
    pallas_call x1, Pallas kernels, token_pass(): pl.pallas_call(functools.partial(token_kernel, lat, heads, tb, tc), grid=...  16.4 us
    all_to_all x1, waiting for transfers between devices, shards(): lax.all_to_all(pair.reshape(chips, rows, wide + STAT), 'chip', 0, 0, tile...  12.8 us
    all_to_all x1, starting transfers between devices, shards(): lax.all_to_all(pair.reshape(chips, rows, wide + STAT), 'chip', 0, 0, tile...  9.47 us
    ppermute x1, starting transfers between devices, shards(): other = lax.ppermute(own, 'core', swap)  5.56 us
    pallas_call x5, Pallas kernels, call(): pl.pallas_call(kernel, out_shape=shapes, in_specs=specs, out_specs=[one]...  4.68 us
    ppermute x3, starting transfers between devices, shards(): lax.ppermute(part, 'head', [(i, (i + k) % groups) for i in range(groups)])  3.64 us
    ppermute x1, starting transfers between devices, shards(): got = lax.ppermute(send, 'core', swap)  3.33 us
  transfers between devices with their start and end apart: 6, of which 5 were waited for; matrix products, arithmetic and copies ran while one was open for 1% of the time, Pallas kernels for 1%

profile of v4, /device:TPU:1, one launch (start us, length us, event | category | flops | bytes accessed | tf_op | source)
XLA Modules:
  0.0 80.0 jit_solution(7438054156624306213)
XLA Ops:
  0.6 0.0 copy-start
  0.7 0.0 copy-start.1
  0.7 0.0 copy-start.2
  0.7 0.0 copy-start.5
  0.7 0.0 copy-start.6
  0.7 0.0 copy-start.3
  0.7 16.4 %token_pass.1 = (bf16[256,640]{1,0:T(8,128)(2,1)}, bf16[256,640]{1,0:T(8,128)(2,1)}, bf16[256,512]{1,0:T(8,128)(2,1)}, bf16[256,128]{1,0:T(8,128)(2,1)}, bf16[256,128]{1,0:T(8,128)(2,1)}) custom-call(s32[1]{0:T(128)} %bitcast.core_ref, f32[2]{0:T(128)} %gamma_ref.1, bf16[8192,256]{1,0:T(8,128)(2,1)} %tok_ref.1, f32[3,8192]{1,0:T(4,128)} %pts_ref.1, ...), custom_call_target="tpu_custom_call" | custom-call | tf_op jit(solution)/shard_map/token_pass/pallas_call | solution.py:185
  17.1 3.3 %collective-permute-start = (bf16[256,640]{1,0:T(8,128)(2,1)}, bf16[256,640]{1,0:T(8,128)(2,1)S(1)}, u32[]{:S(2)}, u32[]{:S(2)}) collective-permute-start(bf16[256,640]{1,0:T(8,128)(2,1)} %get-tuple-element.20), channel_id=1, source_target_pairs={{0,4},{4,0},{1,5},{5,1},{2,6},{6,2},{3,7},{7,3},{8,12},{12,8},{9,1... | collective-permute-start | bytes 983048 | tf_op jit(solution)/shard_map/ppermute | solution.py:371
  20.4 1.1 %convert_element_type.3.a_ref = f32[256,640]{1,0:T(8,128)S(1)} convert(bf16[256,640]{1,0:T(8,128)(2,1)} %get-tuple-element.19) | non-fusion elementwise | flops 163840 | bytes 983040 | tf_op jit(solution)/shard_map/convert_element_type | solution.py:372
  21.5 0.4 collective-permute-done.b_ref
  21.9 1.2 %pair_sum.1 = bf16[256,640]{1,0:T(8,128)(2,1)} custom-call(f32[256,640]{1,0:T(8,128)S(1)} %convert_element_type.3.a_ref, bf16[256,640]{1,0:T(8,128)(2,1)S(1)} %collective-permute-done.b_ref), custom_call_target="tpu_custom_call" | custom-call | flops 400000000 | bytes 1000000 | tf_op jit(solution)/shard_map/pair_sum/pallas_call | solution.py:346
  23.0 9.5 %all-to-all-start = ((bf16[32,8,640]{2,1,0:T(8,128)(2,1)}), bf16[32,8,640]{2,1,0:T(8,128)(2,1)S(1)}, u32[]{:S(2)}, u32[]{:S(2)}) async-start(bf16[32,8,640]{2,1,0:T(8,128)(2,1)} %bitcast.2), calls=%async_computation | async-start | bytes 655360 | tf_op jit(solution)/shard_map/all_to_all | solution.py:373
  32.5 12.8 %all-to-all-done = bf16[32,8,640]{2,1,0:T(8,128)(2,1)S(1)} async-done(((bf16[32,8,640]{2,1,0:T(8,128)(2,1)}), bf16[32,8,640]{2,1,0:T(8,128)(2,1)S(1)}, u32[]{:S(2)}, u32[]{:S(2)}) %all-to-all-start) | async-done | bytes 327712 | tf_op jit(solution)/shard_map/all_to_all | solution.py:373
  45.3 0.0 copy-done
  45.3 0.0 copy-done.1
  45.3 0.0 copy-done.2
  45.3 0.0 copy-done.5
  45.3 0.0 copy-done.6
  45.3 0.7 owner_rows.1
  46.0 2.5 %collective-permute-start.3 = (bf16[8,512]{1,0:T(8,128)(2,1)S(1)}, bf16[8,512]{1,0:T(8,128)(2,1)S(1)}, u32[]{:S(2)}, u32[]{:S(2)}) collective-permute-start(bf16[8,512]{1,0:T(8,128)(2,1)S(1)} %get-tuple-element.21.refs_0_), channel_id=1, source_target_pairs={{0,3},{1,0},{2,1},{3,2},{4,7},{5,4},{6,5},{7,6},{8,11},{9,8},{10,9... | collective-permute-start | bytes 24584 | tf_op jit(solution)/shard_map/ppermute | solution.py:379
  48.5 0.5 collective-permute-start.2
  49.0 0.6 collective-permute-start.1
  49.6 0.0 collective-permute-done.3.refs_3_
  49.6 2.9 %collective-permute-done.2.refs_2_ = bf16[8,512]{1,0:T(8,128)(2,1)S(1)} collective-permute-done((bf16[8,512]{1,0:T(8,128)(2,1)S(1)}, bf16[8,512]{1,0:T(8,128)(2,1)S(1)}, u32[]{:S(2)}, u32[]{:S(2)}) %collective-permute-start.2) | collective-permute-done | bytes 8224 | tf_op jit(solution)/shard_map/ppermute | solution.py:379
  52.5 0.2 collective-permute-done.1.refs_1_
  52.7 0.4 spread_rows.1
  53.2 18.0 %all_to_all.10 = bf16[32,8,1024]{2,1,0:T(8,128)(2,1)S(1)} all-to-all(bf16[32,8,1024]{2,1,0:T(8,128)(2,1)S(1)} %bitcast.8), channel_id=1, replica_groups=mesh['chip'=32,'core'=2,'head'=4] {'chip'}, dimensions={0} | all-to-all | bytes 1048576 | tf_op jit(solution)/shard_map/all_to_all | solution.py:383
  71.2 5.6 %collective-permute-start.4 = (bf16[256,1024]{1,0:T(8,128)(2,1)S(1)}, bf16[256,1024]{1,0:T(8,128)(2,1)S(1)}, u32[]{:S(2)}, u32[]{:S(2)}) collective-permute-start(bf16[256,1024]{1,0:T(8,128)(2,1)S(1)} %bitcast.6), channel_id=1, source_target_pairs={{0,4},{4,0},{1,5},{5,1},{2,6},{6,2},{3,7},{7,3},{8,12},{12,8},{9,1... | collective-permute-start | bytes 1572872 | tf_op jit(solution)/shard_map/ppermute | solution.py:384
  76.7 0.0 copy-done.8
  76.7 0.6 finish_own.1
  77.4 0.9 %collective-permute-done.4.other_ref = bf16[256,1024]{1,0:T(8,128)(2,1)S(1)} collective-permute-done((bf16[256,1024]{1,0:T(8,128)(2,1)S(1)}, bf16[256,1024]{1,0:T(8,128)(2,1)S(1)}, u32[]{:S(2)}, u32[]{:S(2)}) %collective-permute-start.4) | collective-permute-done | bytes 524320 | tf_op jit(solution)/shard_map/ppermute | solution.py:384
  78.3 1.8 %finish.1 = (bf16[256,512]{1,0:T(8,128)(2,1)}, f32[256,512]{1,0:T(8,128)}, f32[512,128]{1,0:T(8,128)}, f32[256,128]{1,0:T(8,128)}, f32[256,128]{1,0:T(8,128)}, /*index=5*/f32[128,512]{1,0:T(8,128)}) custom-call(s32[1]{0:T(128)} %bitcast.core_ref, bf16[256,1024]{1,0:T(8,128)(2,1)S(1)} %collective-permute-done.4.other_ref, bf16[256,128]{1,0:T(8,128)(2,1)S(1)} %copy-done.7, ...), custom_call_target="tpu_custom_call" | custom-call | flops 400000000 | bytes 1000000 | tf_op jit(solution)/shard_map/finish/pallas_call | solution.py:346
  (6 shorter events, 0.0 us)
Async XLA Ops:
  0.6 44.6 %copy-start = (bf16[256,512]{1,0:T(8,128)(2,1)S(1)}, bf16[256,512]{1,0:T(8,128)(2,1)}, u32[]{:S(2)}) copy-start(bf16[256,512]{1,0:T(8,128)(2,1)} %du_ref.5) | copy-start | bytes 786436
  0.7 44.6 %copy-start.1 = (bf16[256,128]{1,0:T(8,128)(2,1)S(1)}, bf16[256,128]{1,0:T(8,128)(2,1)}, u32[]{:S(2)}) copy-start(bf16[256,128]{1,0:T(8,128)(2,1)} %wk_ref.7) | copy-start | bytes 196612
  0.7 44.6 %copy-start.2 = (bf16[256,128]{1,0:T(8,128)(2,1)S(1)}, bf16[256,128]{1,0:T(8,128)(2,1)}, u32[]{:S(2)}) copy-start(bf16[256,128]{1,0:T(8,128)(2,1)} %wv_ref.7) | copy-start | bytes 196612
  0.7 44.6 %copy-start.5 = (bf16[512,128]{1,0:T(8,128)(2,1)S(1)}, bf16[512,128]{1,0:T(8,128)(2,1)}, u32[]{:S(2)}) copy-start(bf16[512,128]{1,0:T(8,128)(2,1)} %wq_ref.3) | copy-start | bytes 393220
  0.7 44.6 %copy-start.6 = (bf16[128,512]{1,0:T(8,128)(2,1)S(1)}, bf16[128,512]{1,0:T(8,128)(2,1)}, u32[]{:S(2)}) copy-start(bf16[128,512]{1,0:T(8,128)(2,1)} %wo_ref.3) | copy-start | bytes 393220
  0.7 52.1 %copy-start.3 = (bf16[256,512]{1,0:T(8,128)(2,1)S(1)}, bf16[256,512]{1,0:T(8,128)(2,1)}, u32[]{:S(2)}) copy-start(bf16[256,512]{1,0:T(8,128)(2,1)} %refs_5_.1) | copy-start | bytes 786436
  17.1 59.7 %copy-start.7 = (bf16[256,128]{1,0:T(8,128)(2,1)S(1)}, bf16[256,128]{1,0:T(8,128)(2,1)}, u32[]{:S(2)}) copy-start(bf16[256,128]{1,0:T(8,128)(2,1)} %get-tuple-element.23.q_ref) | copy-start | bytes 196612
  17.1 59.7 %copy-start.8 = (bf16[256,128]{1,0:T(8,128)(2,1)S(1)}, bf16[256,128]{1,0:T(8,128)(2,1)}, u32[]{:S(2)}) copy-start(bf16[256,128]{1,0:T(8,128)(2,1)} %get-tuple-element.24.do_ref) | copy-start | bytes 196612
  17.1 4.8 %collective-permute-start = (bf16[256,640]{1,0:T(8,128)(2,1)}, bf16[256,640]{1,0:T(8,128)(2,1)S(1)}, u32[]{:S(2)}, u32[]{:S(2)}) collective-permute-start(bf16[256,640]{1,0:T(8,128)(2,1)} %get-tuple-element.20), channel_id=1, source_target_pairs={{0,4},{4,0},{1,5},{5,1},{2,6},{6,2},{3,7},{7,3},{8,12},{12,8},{9,1... | collective-permute-start | bytes 983048 | tf_op jit(solution)/shard_map/ppermute | solution.py:371
  20.4 57.9 %copy-start.4 = (bf16[256,512]{1,0:T(8,128)(2,1)S(1)}, bf16[256,512]{1,0:T(8,128)(2,1)}, u32[]{:S(2)}) copy-start(bf16[256,512]{1,0:T(8,128)(2,1)} %get-tuple-element.25.latn_ref) | copy-start | bytes 786436
  23.0 22.2 %all-to-all-start = ((bf16[32,8,640]{2,1,0:T(8,128)(2,1)}), bf16[32,8,640]{2,1,0:T(8,128)(2,1)S(1)}, u32[]{:S(2)}, u32[]{:S(2)}) async-start(bf16[32,8,640]{2,1,0:T(8,128)(2,1)} %bitcast.2), calls=%async_computation | async-start | bytes 655360 | tf_op jit(solution)/shard_map/all_to_all | solution.py:373
  46.0 3.6 %collective-permute-start.3 = (bf16[8,512]{1,0:T(8,128)(2,1)S(1)}, bf16[8,512]{1,0:T(8,128)(2,1)S(1)}, u32[]{:S(2)}, u32[]{:S(2)}) collective-permute-start(bf16[8,512]{1,0:T(8,128)(2,1)S(1)} %get-tuple-element.21.refs_0_), channel_id=1, source_target_pairs={{0,3},{1,0},{2,1},{3,2},{4,7},{5,4},{6,5},{7,6},{8,11},{9,8},{10,9... | collective-permute-start | bytes 24584 | tf_op jit(solution)/shard_map/ppermute | solution.py:379
  48.5 4.0 %collective-permute-start.2 = (bf16[8,512]{1,0:T(8,128)(2,1)S(1)}, bf16[8,512]{1,0:T(8,128)(2,1)S(1)}, u32[]{:S(2)}, u32[]{:S(2)}) collective-permute-start(bf16[8,512]{1,0:T(8,128)(2,1)S(1)} %get-tuple-element.21.refs_0_), channel_id=1, source_target_pairs={{0,2},{1,3},{2,0},{3,1},{4,6},{5,7},{6,4},{7,5},{8,10},{9,11},{10,... | collective-permute-start | bytes 24584 | tf_op jit(solution)/shard_map/ppermute | solution.py:379
  49.0 3.7 %collective-permute-start.1 = (bf16[8,512]{1,0:T(8,128)(2,1)S(1)}, bf16[8,512]{1,0:T(8,128)(2,1)S(1)}, u32[]{:S(2)}, u32[]{:S(2)}) collective-permute-start(bf16[8,512]{1,0:T(8,128)(2,1)S(1)} %get-tuple-element.21.refs_0_), channel_id=1, source_target_pairs={{0,1},{1,2},{2,3},{3,0},{4,5},{5,6},{6,7},{7,4},{8,9},{9,10},{10,1... | collective-permute-start | bytes 24584 | tf_op jit(solution)/shard_map/ppermute | solution.py:379
  71.2 7.1 %collective-permute-start.4 = (bf16[256,1024]{1,0:T(8,128)(2,1)S(1)}, bf16[256,1024]{1,0:T(8,128)(2,1)S(1)}, u32[]{:S(2)}, u32[]{:S(2)}) collective-permute-start(bf16[256,1024]{1,0:T(8,128)(2,1)S(1)} %bitcast.6), channel_id=1, source_target_pairs={{0,4},{4,0},{1,5},{5,1},{2,6},{6,2},{3,7},{7,3},{8,12},{12,8},{9,1... | collective-permute-start | bytes 1572872 | tf_op jit(solution)/shard_map/ppermute | solution.py:384

commit v5 on v4

--- a/solution.py
+++ b/solution.py
@@ -56,8 +56,14 @@
     return high + (v - high).astype(bf16).astype(f32)
 
 
+def projections(lat_ref, du_ref, wq_ref, wo_ref):
+    latn = norm_rows(lat_ref[...].astype(f32)).astype(bf16)
+    q = (nn(latn, wq_ref[...]) * (HS ** -0.5)).astype(bf16)
+    return latn, q, nt(du_ref[...], wo_ref[...]).astype(bf16)
+
+
 def token_kernel(lat, heads, tb, tc, core_ref, gamma_ref, tok_ref, pts_ref, lat_ref, anc_ref, wq_ref, wk_ref, wv_ref,
-                 wo_ref, du_ref, send_ref, keep_ref, latn_out, q_out, do_out,
+                 wo_ref, du_ref, send_ref, keep_ref,
                  anc_s, p_s, r_s, shift_s, x_s, acc_s, z_s):
     step = pl.program_id(0)
     steps = pl.num_programs(0)
@@ -66,12 +72,7 @@
 
     @pl.when(step == 0)
     def _():
-        latn = norm_rows(lat_ref[...].astype(f32)).astype(bf16)
-        latn_out[...] = latn
-        q = (nn(latn, wq_ref[...]) * (HS ** -0.5)).astype(bf16)
-        do = nt(du_ref[...], wo_ref[...]).astype(bf16)
-        q_out[...] = q
-        do_out[...] = do
+        _, q, do = projections(lat_ref, du_ref, wq_ref, wo_ref)
         box = jnp.zeros((lat, 1), f32)
         for k in range(3):
             a = column(anc_ref[k:k + 1, :], lat)
@@ -179,7 +180,7 @@
         return pl.BlockSpec(a.shape, lambda i: (0,) * len(a.shape))
 
     smem = pl.BlockSpec(memory_space=pltpu.SMEM)
-    shapes = [(rows // 2, cols)] * 2 + [(lat, dl), (lat, width), (lat, width)]
+    shapes = [(rows // 2, cols)] * 2
     outs = [jax.ShapeDtypeStruct(s, bf16) for s in shapes]
     held = (coords, latents, anchors, wq, wk, wv, wo, du)
     return pl.pallas_call(
@@ -285,8 +286,8 @@
         out_ref[s * 2 * rows:(s + 1) * 2 * rows, :] = block
 
 
-def half_terms(chips, heads, core, rows_ref, q_ref, do_ref, wk_ref, wv_ref):
-    lat, width = q_ref.shape
+def half_terms(chips, heads, core, rows_ref, q_all, do_all, wk_ref, wv_ref):
+    lat, width = q_all.shape
     feat = wk_ref.shape[0]
     half = rows_ref.shape[0]
     rows = half // chips
@@ -301,8 +302,8 @@
     spread = one_hot(latent(iota((half, lat), 0)) == iota((half, lat), 1))
     mine = iota((half, width), 0) % rows // per == iota((half, width), 1) // HS
     zero = jnp.zeros((), f32)
-    do = jnp.where(mine, nn(spread, do_ref[...]), zero).astype(bf16)
-    q = jnp.where(mine, nn(spread, q_ref[...]), zero).astype(bf16)
+    do = jnp.where(mine, nn(spread, do_all), zero).astype(bf16)
+    q = jnp.where(mine, nn(spread, q_all), zero).astype(bf16)
     o = jnp.where(mine, nn(f, wv_ref[...]), zero).astype(bf16)
     dq = jnp.where(mine, nn(g, wk_ref[...]) * (HS ** -0.5), zero).astype(bf16)
     at = iota((lat, half), 1)
@@ -319,15 +320,17 @@
     )
 
 
-def finish_own_kernel(chips, heads, core_ref, own_ref, q_ref, do_ref, wk_ref, wv_ref, *outs):
-    for out, term in zip(outs, half_terms(chips, heads, core_ref[0], own_ref, q_ref, do_ref, wk_ref, wv_ref)):
+def finish_own_kernel(chips, heads, core_ref, own_ref, lat_ref, du_ref, wq_ref, wo_ref, wk_ref, wv_ref, *outs):
+    latn, q, do = projections(lat_ref, du_ref, wq_ref, wo_ref)
+    terms = (latn, q, do) + half_terms(chips, heads, core_ref[0], own_ref, q, do, wk_ref, wv_ref)
+    for out, term in zip(outs, terms):
         out[...] = term
 
 
-def finish_kernel(chips, heads, core_ref, other_ref, q_ref, do_ref, wk_ref, wv_ref, latn_ref, du_ref,
+def finish_kernel(chips, heads, core_ref, other_ref, wk_ref, wv_ref, du_ref, latn_ref, q_ref, do_ref,
                   dwv_ref, dwk_ref, o_ref, dq_ref, up_ref, dl_ref,
                   up_out, dl_out, dwq_out, dwk_out, dwv_out, dwo_out):
-    dwv, dwk, o, dq, up, dl = half_terms(chips, heads, 1 - core_ref[0], other_ref, q_ref, do_ref, wk_ref, wv_ref)
+    dwv, dwk, o, dq, up, dl = half_terms(chips, heads, 1 - core_ref[0], other_ref, q_ref[...], do_ref[...], wk_ref, wv_ref)
     dwv_out[...] = dwv_ref[...] + dwv
     dwk_out[...] = dwk_ref[...] + dwk
     up_out[...] = up_ref[...] + up
@@ -365,7 +368,7 @@
     chip = lax.axis_index("chip").astype(jnp.int32).reshape(1)
     swap = [(0, 1), (1, 0)]
 
-    send, keep, latn, q, do = token_pass(
+    send, keep = token_pass(
         core, gamma, tokens, coords, latents, anchors, w_query, w_key, w_value, w_out, d_update
     )
     got = lax.ppermute(send, "core", swap)
@@ -382,14 +385,14 @@
     )(core, chip, *parts, fg, latents)
     own = lax.all_to_all(copies.reshape(chips, rows, wide + dl), "chip", 0, 0, tiled=True).reshape(half, wide + dl)
     other = lax.ppermute(own, "core", swap)
-    terms = [((feat, width), f32)] * 2 + [((lat, width), bf16)] * 2 + [((lat, dl), bf16), ((lat, dl), f32)]
+    terms = [((lat, dl), bf16), ((lat, width), bf16), ((lat, width), bf16)] + [((feat, width), f32)] * 2 + [((lat, width), bf16)] * 2 + [((lat, dl), bf16), ((lat, dl), f32)]
     mine = small(functools.partial(finish_own_kernel, chips, heads), terms, 1, "finish_own")(
-        core, own, q, do, w_key, w_value
+        core, own, latents, d_update, w_query, w_out, w_key, w_value
     )
     outs = [((lat, dl), bf16), ((lat, dl), f32), ((dl, width), f32), ((feat, width), f32), ((feat, width), f32), ((width, dl), f32)]
     return tuple(
         small(functools.partial(finish_kernel, chips, heads), outs, 1, "finish")(
-            core, other, q, do, w_key, w_value, latn, d_update, *mine
+            core, other, w_key, w_value, d_update, *mine
         )
     )
 

time: 80.3 us -> 80 us (level)
  transfers between devices with their start and end apart: 6 -> 6, of which waited for: 5 -> 5; matrix products, arithmetic and copies ran while one was open for 1% -> 1% of each run, Pallas kernels for 1% -> 2%
where the time goes in v5:
time: 80 us; the launch traced here: 79.8 us
  starting transfers between devices  21.9 us (27%)
  Pallas kernels  21.5 us (27%)
  blocking collectives  18 us (22%)
  waiting for transfers between devices  16.6 us (21%)
  other arithmetic  1.02 us (1%)
    all_to_all x1, blocking collectives, shards(): lax.all_to_all(copies.reshape(chips, rows, wide + dl), 'chip', 0, 0, tile...  18 us
    pallas_call x1, Pallas kernels, token_pass(): pl.pallas_call(functools.partial(token_kernel, lat, heads, tb, tc), grid=...  16.2 us
    all_to_all x1, waiting for transfers between devices, shards(): lax.all_to_all(pair.reshape(chips, rows, wide + STAT), 'chip', 0, 0, tile...  12.8 us
    all_to_all x1, starting transfers between devices, shards(): lax.all_to_all(pair.reshape(chips, rows, wide + STAT), 'chip', 0, 0, tile...  9.47 us
    ppermute x1, starting transfers between devices, shards(): other = lax.ppermute(own, 'core', swap)  5.56 us
    pallas_call x5, Pallas kernels, call(): pl.pallas_call(kernel, out_shape=shapes, in_specs=specs, out_specs=[one]...  5.24 us
    ppermute x3, starting transfers between devices, shards(): lax.ppermute(part, 'head', [(i, (i + k) % groups) for i in range(groups)])  3.63 us
    ppermute x1, starting transfers between devices, shards(): got = lax.ppermute(send, 'core', swap)  3.24 us
  transfers between devices with their start and end apart: 6, of which 5 were waited for; matrix products, arithmetic and copies ran while one was open for 1% of the time, Pallas kernels for 2%

profile of v5, /device:TPU:1, one launch (start us, length us, event | category | flops | bytes accessed | tf_op | source)
XLA Modules:
  0.0 79.8 jit_solution(12296773519090520814)
XLA Ops:
  0.6 0.0 copy-start
  0.7 0.0 copy-start.1
  0.7 0.0 copy-start.2
  0.7 0.0 copy-start.4
  0.7 0.0 copy-start.5
  0.7 0.0 copy-start.3
  0.7 16.2 %token_pass.1 = (bf16[256,640]{1,0:T(8,128)(2,1)}, bf16[256,640]{1,0:T(8,128)(2,1)}) custom-call(s32[1]{0:T(128)} %bitcast.core_ref, f32[2]{0:T(128)} %gamma_ref.1, bf16[8192,256]{1,0:T(8,128)(2,1)} %tok_ref.1, f32[3,8192]{1,0:T(4,128)} %pts_ref.1, bf16[256,512]{1,0:T(8,128)(2,1)} %lat_ref.3, f32[3,256]{1,0:T(4,128)} %anc_ref.1, bf16[512,128]{1,0:T(8,128)(2,1)} %wq_ref.5, ...), custom_call_target="tpu_custom_call" | custom-call | tf_op jit(solution)/shard_map/token_pass/pallas_call | solution.py:186
  16.9 3.2 %collective-permute-start = (bf16[256,640]{1,0:T(8,128)(2,1)}, bf16[256,640]{1,0:T(8,128)(2,1)S(1)}, u32[]{:S(2)}, u32[]{:S(2)}) collective-permute-start(bf16[256,640]{1,0:T(8,128)(2,1)} %get-tuple-element.20), channel_id=1, source_target_pairs={{0,4},{4,0},{1,5},{5,1},{2,6},{6,2},{3,7},{7,3},{8,12},{12,8},{9,1... | collective-permute-start | bytes 983048 | tf_op jit(solution)/shard_map/ppermute | solution.py:374
  20.2 1.0 %convert_element_type.3.a_ref = f32[256,640]{1,0:T(8,128)S(1)} convert(bf16[256,640]{1,0:T(8,128)(2,1)} %get-tuple-element.19) | non-fusion elementwise | flops 163840 | bytes 983040 | tf_op jit(solution)/shard_map/convert_element_type | solution.py:375
  21.2 0.4 collective-permute-done.b_ref
  21.6 1.2 %pair_sum.1 = bf16[256,640]{1,0:T(8,128)(2,1)} custom-call(f32[256,640]{1,0:T(8,128)S(1)} %convert_element_type.3.a_ref, bf16[256,640]{1,0:T(8,128)(2,1)S(1)} %collective-permute-done.b_ref), custom_call_target="tpu_custom_call" | custom-call | flops 400000000 | bytes 1000000 | tf_op jit(solution)/shard_map/pair_sum/pallas_call | solution.py:349
  22.8 9.5 %all-to-all-start = ((bf16[32,8,640]{2,1,0:T(8,128)(2,1)}), bf16[32,8,640]{2,1,0:T(8,128)(2,1)S(1)}, u32[]{:S(2)}, u32[]{:S(2)}) async-start(bf16[32,8,640]{2,1,0:T(8,128)(2,1)} %bitcast.2), calls=%async_computation | async-start | bytes 655360 | tf_op jit(solution)/shard_map/all_to_all | solution.py:376
  32.3 12.8 %all-to-all-done = bf16[32,8,640]{2,1,0:T(8,128)(2,1)S(1)} async-done(((bf16[32,8,640]{2,1,0:T(8,128)(2,1)}), bf16[32,8,640]{2,1,0:T(8,128)(2,1)S(1)}, u32[]{:S(2)}, u32[]{:S(2)}) %all-to-all-start) | async-done | bytes 327712 | tf_op jit(solution)/shard_map/all_to_all | solution.py:376
  45.0 0.0 copy-done
  45.0 0.0 copy-done.1
  45.0 0.0 copy-done.2
  45.1 0.0 copy-done.4
  45.1 0.0 copy-done.5
  45.1 0.7 owner_rows.1
  45.8 2.5 %collective-permute-start.3 = (bf16[8,512]{1,0:T(8,128)(2,1)S(1)}, bf16[8,512]{1,0:T(8,128)(2,1)S(1)}, u32[]{:S(2)}, u32[]{:S(2)}) collective-permute-start(bf16[8,512]{1,0:T(8,128)(2,1)S(1)} %get-tuple-element.21.refs_0_), channel_id=1, source_target_pairs={{0,3},{1,0},{2,1},{3,2},{4,7},{5,4},{6,5},{7,6},{8,11},{9,8},{10,9... | collective-permute-start | bytes 24584 | tf_op jit(solution)/shard_map/ppermute | solution.py:382
  48.3 0.5 collective-permute-start.2
  48.8 0.6 collective-permute-start.1
  49.4 0.0 collective-permute-done.3.refs_3_
  49.4 2.9 %collective-permute-done.2.refs_2_ = bf16[8,512]{1,0:T(8,128)(2,1)S(1)} collective-permute-done((bf16[8,512]{1,0:T(8,128)(2,1)S(1)}, bf16[8,512]{1,0:T(8,128)(2,1)S(1)}, u32[]{:S(2)}, u32[]{:S(2)}) %collective-permute-start.2) | collective-permute-done | bytes 8224 | tf_op jit(solution)/shard_map/ppermute | solution.py:382
  52.3 0.2 collective-permute-done.1.refs_1_
  52.5 0.0 copy-done.3
  52.5 0.4 spread_rows.1
  52.9 18.0 %all_to_all.10 = bf16[32,8,1024]{2,1,0:T(8,128)(2,1)S(1)} all-to-all(bf16[32,8,1024]{2,1,0:T(8,128)(2,1)S(1)} %bitcast.8), channel_id=1, replica_groups=mesh['chip'=32,'core'=2,'head'=4] {'chip'}, dimensions={0} | all-to-all | bytes 1048576 | tf_op jit(solution)/shard_map/all_to_all | solution.py:386
  70.9 5.6 %collective-permute-start.4 = (bf16[256,1024]{1,0:T(8,128)(2,1)S(1)}, bf16[256,1024]{1,0:T(8,128)(2,1)S(1)}, u32[]{:S(2)}, u32[]{:S(2)}) collective-permute-start(bf16[256,1024]{1,0:T(8,128)(2,1)S(1)} %bitcast.6), channel_id=1, source_target_pairs={{0,4},{4,0},{1,5},{5,1},{2,6},{6,2},{3,7},{7,3},{8,12},{12,8},{9,1... | collective-permute-start | bytes 1572872 | tf_op jit(solution)/shard_map/ppermute | solution.py:387
  76.5 1.2 %finish_own.1 = (bf16[256,512]{1,0:T(8,128)(2,1)S(1)}, bf16[256,128]{1,0:T(8,128)(2,1)S(1)}, bf16[256,128]{1,0:T(8,128)(2,1)S(1)}, f32[256,128]{1,0:T(8,128)S(1)...) custom-call(s32[1]{0:T(128)} %bitcast.core_ref, ...), custom_call_target="tpu_custom_call" | custom-call | flops 400000000 | bytes 1000000 | tf_op jit(solution)/shard_map/finish_own/pallas_call | solution.py:349
  77.7 0.3 collective-permute-done.4.other_ref
  78.0 1.8 %finish.1 = (bf16[256,512]{1,0:T(8,128)(2,1)}, f32[256,512]{1,0:T(8,128)}, f32[512,128]{1,0:T(8,128)}, f32[256,128]{1,0:T(8,128)}, f32[256,128]{1,0:T(8,128)}, /*index=5*/f32[128,512]{1,0:T(8,128)}) custom-call(s32[1]{0:T(128)} %bitcast.core_ref, bf16[256,1024]{1,0:T(8,128)(2,1)S(1)} %collective-permute-done.4.other_ref, bf16[256,128]{1,0:T(8,128)(2,1)S(1)} %copy-done.1, ...), custom_call_target="tpu_custom_call" | custom-call | flops 400000000 | bytes 1000000 | tf_op jit(solution)/shard_map/finish/pallas_call | solution.py:349
Async XLA Ops:
  0.6 44.4 %copy-start = (bf16[256,512]{1,0:T(8,128)(2,1)S(1)}, bf16[256,512]{1,0:T(8,128)(2,1)}, u32[]{:S(2)}) copy-start(bf16[256,512]{1,0:T(8,128)(2,1)} %du_ref.7) | copy-start | bytes 786436
  0.7 44.4 %copy-start.1 = (bf16[256,128]{1,0:T(8,128)(2,1)S(1)}, bf16[256,128]{1,0:T(8,128)(2,1)}, u32[]{:S(2)}) copy-start(bf16[256,128]{1,0:T(8,128)(2,1)} %wk_ref.7) | copy-start | bytes 196612
  0.7 44.4 %copy-start.2 = (bf16[256,128]{1,0:T(8,128)(2,1)S(1)}, bf16[256,128]{1,0:T(8,128)(2,1)}, u32[]{:S(2)}) copy-start(bf16[256,128]{1,0:T(8,128)(2,1)} %wv_ref.7) | copy-start | bytes 196612
  0.7 44.4 %copy-start.4 = (bf16[512,128]{1,0:T(8,128)(2,1)S(1)}, bf16[512,128]{1,0:T(8,128)(2,1)}, u32[]{:S(2)}) copy-start(bf16[512,128]{1,0:T(8,128)(2,1)} %wq_ref.5) | copy-start | bytes 393220
  0.7 44.4 %copy-start.5 = (bf16[128,512]{1,0:T(8,128)(2,1)S(1)}, bf16[128,512]{1,0:T(8,128)(2,1)}, u32[]{:S(2)}) copy-start(bf16[128,512]{1,0:T(8,128)(2,1)} %wo_ref.5) | copy-start | bytes 393220
  0.7 51.8 %copy-start.3 = (bf16[256,512]{1,0:T(8,128)(2,1)S(1)}, bf16[256,512]{1,0:T(8,128)(2,1)}, u32[]{:S(2)}) copy-start(bf16[256,512]{1,0:T(8,128)(2,1)} %lat_ref.3) | copy-start | bytes 786436
  16.9 4.7 %collective-permute-start = (bf16[256,640]{1,0:T(8,128)(2,1)}, bf16[256,640]{1,0:T(8,128)(2,1)S(1)}, u32[]{:S(2)}, u32[]{:S(2)}) collective-permute-start(bf16[256,640]{1,0:T(8,128)(2,1)} %get-tuple-element.20), channel_id=1, source_target_pairs={{0,4},{4,0},{1,5},{5,1},{2,6},{6,2},{3,7},{7,3},{8,12},{12,8},{9,1... | collective-permute-start | bytes 983048 | tf_op jit(solution)/shard_map/ppermute | solution.py:374
  22.8 22.2 %all-to-all-start = ((bf16[32,8,640]{2,1,0:T(8,128)(2,1)}), bf16[32,8,640]{2,1,0:T(8,128)(2,1)S(1)}, u32[]{:S(2)}, u32[]{:S(2)}) async-start(bf16[32,8,640]{2,1,0:T(8,128)(2,1)} %bitcast.2), calls=%async_computation | async-start | bytes 655360 | tf_op jit(solution)/shard_map/all_to_all | solution.py:376
  45.8 3.6 %collective-permute-start.3 = (bf16[8,512]{1,0:T(8,128)(2,1)S(1)}, bf16[8,512]{1,0:T(8,128)(2,1)S(1)}, u32[]{:S(2)}, u32[]{:S(2)}) collective-permute-start(bf16[8,512]{1,0:T(8,128)(2,1)S(1)} %get-tuple-element.21.refs_0_), channel_id=1, source_target_pairs={{0,3},{1,0},{2,1},{3,2},{4,7},{5,4},{6,5},{7,6},{8,11},{9,8},{10,9... | collective-permute-start | bytes 24584 | tf_op jit(solution)/shard_map/ppermute | solution.py:382
  48.3 4.0 %collective-permute-start.2 = (bf16[8,512]{1,0:T(8,128)(2,1)S(1)}, bf16[8,512]{1,0:T(8,128)(2,1)S(1)}, u32[]{:S(2)}, u32[]{:S(2)}) collective-permute-start(bf16[8,512]{1,0:T(8,128)(2,1)S(1)} %get-tuple-element.21.refs_0_), channel_id=1, source_target_pairs={{0,2},{1,3},{2,0},{3,1},{4,6},{5,7},{6,4},{7,5},{8,10},{9,11},{10,... | collective-permute-start | bytes 24584 | tf_op jit(solution)/shard_map/ppermute | solution.py:382
  48.8 3.7 %collective-permute-start.1 = (bf16[8,512]{1,0:T(8,128)(2,1)S(1)}, bf16[8,512]{1,0:T(8,128)(2,1)S(1)}, u32[]{:S(2)}, u32[]{:S(2)}) collective-permute-start(bf16[8,512]{1,0:T(8,128)(2,1)S(1)} %get-tuple-element.21.refs_0_), channel_id=1, source_target_pairs={{0,1},{1,2},{2,3},{3,0},{4,5},{5,6},{6,7},{7,4},{8,9},{9,10},{10,1... | collective-permute-start | bytes 24584 | tf_op jit(solution)/shard_map/ppermute | solution.py:382
  70.9 7.1 %collective-permute-start.4 = (bf16[256,1024]{1,0:T(8,128)(2,1)S(1)}, bf16[256,1024]{1,0:T(8,128)(2,1)S(1)}, u32[]{:S(2)}, u32[]{:S(2)}) collective-permute-start(bf16[256,1024]{1,0:T(8,128)(2,1)S(1)} %bitcast.6), channel_id=1, source_target_pairs={{0,4},{4,0},{1,5},{5,1},{2,6},{6,2},{3,7},{7,3},{8,12},{12,8},{9,1... | collective-permute-start | bytes 1572872 | tf_op jit(solution)/shard_map/ppermute | solution.py:387
